TPU v7x, 32 devices: a whole 2x2x4 slice. The times are simulated.
32 devices in a mesh: dp: 16 (over z, y, x), expert: 2 (over core).
Axes of the slice: x: 2, y: 2, z: 4, core: 2. Of those that a mesh axis runs over, the one named last changes fastest.
Arguments:
- tokens: bfloat16 [6144, 4096], P('dp'), may hold values from -8 to 8, as said below
- centroids: bfloat16 [512, 4096], P('expert'), may hold values from -8 to 8, as said below
- prices: float32 [512], P('expert'), may hold values from 0 to 259.9922, as said below
- epsilon: float32 [1], replicated, may hold values from 0.125 to 1, as said below
Outputs:
- final_prices: float32 [512], P('expert')
- best_expert: int32 [6144], P('dp')
- holder: int32 [512], P('expert')
- refreshed: bfloat16 [512, 4096], P('expert')
Inputs may be any that keep to these rules, and one draw needn't show every extreme that they name: `tokens`: every entry is a whole number. `centroids`: every entry is a whole number. `prices`: distinct multiples of 1/128. `epsilon`: A multiple of 1/8.
All inputs are finite; a program needn't handle non-finite values.
Results may differ from a plain program's by a relative error of at most 0.001.
Values may be sent and summed in bfloat16 or wider, within the bound.
No kernel may reach another device: no remote copies, remote signals or barrier semaphores. Data moves between devices by JAX's collectives and lax.ppermute only.
A program may use at most 64 MiB of HBM per device.

v0:
```python
import jax
import jax.numpy as jnp
from jax import lax
from jax.sharding import PartitionSpec as P

ROUNDS = 3


lowest = -1e30
far_index = 1 << 30
far_float = 1073741824.0


def merged(value, axis, join):
    pieces = jax.tree.map(lambda part: lax.all_gather(part, axis), value)
    head = jax.tree.map(lambda part: part[0], pieces)
    tail = jax.tree.map(lambda part: part[1:], pieces)
    total, _ = lax.scan(lambda total, section: (join(total, section), None), head, tail)
    return total


def local_top(values, expert_ids):
    best_value = jnp.max(values, axis=0)
    best_index = jnp.min(
        jnp.where(values == best_value[None, :], expert_ids[:, None], far_index), axis=0
    )
    second_value = jnp.max(
        jnp.where(expert_ids[:, None] == best_index[None, :], lowest, values), axis=0
    )
    return (best_value, best_index, second_value)


def choose_first(earlier, later):
    left_value, left_index, left_second = earlier
    right_value, right_index, right_second = later
    take_left = (left_value > right_value) | (left_value == right_value) & (
        left_index < right_index
    )
    best_value = jnp.where(take_left, left_value, right_value)
    best_index = jnp.where(take_left, left_index, right_index)
    second_value = jnp.where(
        take_left, jnp.maximum(left_second, right_value), jnp.maximum(right_second, left_value)
    )
    return (best_value, best_index, second_value)


def body(tokens, centroids, prices, epsilon):
    local_experts = centroids.shape[0]
    local_tokens = tokens.shape[0]
    scores = (
        lax.dot_general(
            centroids, tokens, (((1,), (1,)), ((), ())), preferred_element_type=jnp.float32
        )
        * 0.015625
    )
    expert_ids = lax.axis_index("expert") * local_experts + jnp.arange(
        local_experts, dtype=jnp.int32
    )
    token_ids = lax.axis_index("dp") * local_tokens + jnp.arange(local_tokens, dtype=jnp.int32)
    token_floats = token_ids.astype(jnp.float32)
    current = prices
    for auction_step in range(ROUNDS):
        values = scores - current[:, None]
        best_value, local_index, second_value = local_top(values, expert_ids)
        index_float = local_index.astype(jnp.float32)
        best_value, index_float, second_value = merged(
            (best_value, index_float, second_value), "expert", choose_first
        )
        best_index = index_float.astype(jnp.int32)
        bids_now = best_value - second_value + epsilon[0]
        claims = expert_ids[:, None] == best_index[None, :]
        local_bid = jnp.max(jnp.where(claims, bids_now[None, :], -1.0), axis=1)
        top_bid = lax.pmax(local_bid, "dp")
        local_first = jnp.min(
            jnp.where(
                claims & (bids_now[None, :] == top_bid[:, None]), token_floats[None, :], far_float
            ),
            axis=1,
        )
        first_float = lax.pmin(local_first, "dp")
        current = current + jnp.maximum(top_bid, 0.0)
        holder = jnp.where(top_bid > 0, first_float, -1.0).astype(jnp.int32)
    local_sums = jnp.dot(claims.astype(jnp.bfloat16), tokens, preferred_element_type=jnp.float32)
    local_counts = jnp.sum(claims, axis=1).astype(jnp.float32)
    feature_sums, counts = lax.psum((local_sums, local_counts), "dp")
    refreshed = (
        0.5 * centroids.astype(jnp.float32) + 0.5 * feature_sums / jnp.maximum(counts, 1.0)[:, None]
    ).astype(jnp.bfloat16)
    return (current, best_index, holder, refreshed)


def solution(mesh):
    placed = (P("dp", None), P("expert", None), P("expert"), P())
    return jax.shard_map(
        body,
        mesh=mesh,
        in_specs=placed,
        out_specs=(P("expert"), P("dp"), P("expert"), P("expert", None)),
        check_vma=False,
    )
```

profile of v0, /device:TPU:0, one launch (start us, length us, event | category | flops | bytes accessed | tf_op | source)
XLA Modules:
  0.0 291.5 jit_solution(14520257070116613939)
XLA Ops:
  7.2 0.0 copy-start
  7.2 0.0 copy-start.3
  7.2 0.0 all-reduce.2.cloned.1.call-start
  7.3 1.8 copy-done
  9.1 2.9 subtract_reduce_fusion.2
  11.9 0.0 copy-done.3
  12.0 0.1 select_reduce_fusion.8
  12.1 0.1 select_reduce_fusion.7
  12.9 1.9 all-gather.9
  14.8 1.8 all-gather.10
  16.6 1.8 all-gather.11
  18.5 0.2 select_reduce_fusion.6
  18.6 43.3 %pmax.21 = f32[256]{0:T(256)S(1)} all-reduce(f32[256]{0:T(256)S(1)} %select_reduce_fusion.6), channel_id=1, replica_groups=mesh['dp'=16,'expert'=2] {'dp'}, use_global_device_ids=true, to_apply=%region_4.5 | all-reduce | flops 256 | bytes 2048 | tf_op jit(solution)/shard_map/pmax | solution.py:73
  62.0 0.1 subtract_reduce_fusion.1
  62.1 0.1 select_reduce_fusion.5
  62.3 0.1 select_reduce_fusion.4
  62.4 1.8 all-gather.12
  64.2 1.8 all-gather.13
  66.0 1.8 all-gather.14
  67.8 0.2 select_reduce_fusion.3
  68.0 36.6 %pmax.22 = f32[256]{0:T(256)S(1)} all-reduce(f32[256]{0:T(256)S(1)} %select_reduce_fusion.3), channel_id=1, replica_groups=mesh['dp'=16,'expert'=2] {'dp'}, use_global_device_ids=true, to_apply=%region_9.10 | all-reduce | flops 256 | bytes 2048 | tf_op jit(solution)/shard_map/pmax | solution.py:73
  104.6 0.0 copy-start.1
  104.6 0.1 subtract_reduce_fusion
  104.7 0.1 select_reduce_fusion.2
  104.9 0.0 copy-start.2
  104.9 1.8 all-gather.15
  106.7 0.0 copy-done.1
  106.7 1.8 all-gather.16
  108.5 0.0 copy-done.2
  108.5 0.6 fusion.19
  109.0 3.3 %fusion = f32[256,4096]{1,0:T(8,128)} fusion(bf16[384,4096]{1,0:T(8,128)(2,1)S(1)} %copy-done, s32[384]{0:T(512)S(1)} %get-tuple-element.57, s32[256]{0:T(256)S(1)} %iota_add_fusion), kind=kOutput, calls=%fused_computation.3 | convolution fusion | flops 805404672 | bytes 7342592 | tf_op jit(solution)/shard_map/dot_general | solution.py:83
  112.3 0.0 all-reduce.2.cloned.1.call-update
  112.3 0.8 select_reduce_fusion.1
  113.2 0.2 fusion.3
  113.4 1.8 all-gather.17
  115.2 0.7 add_reduce_fusion
  115.9 0.2 fusion.2
  116.1 40.5 %pmax.23 = f32[256]{0:T(256)S(1)} all-reduce(f32[256]{0:T(256)S(1)} %fusion.2), channel_id=1, replica_groups=mesh['dp'=16,'expert'=2] {'dp'}, use_global_device_ids=true, to_apply=%region_14.15 | all-reduce | flops 256 | bytes 2048 | tf_op jit(solution)/shard_map/pmax | solution.py:73
  156.6 0.2 select_reduce_fusion
  156.8 37.2 %pmin.7 = f32[256]{0:T(256)S(1)} all-reduce(f32[256]{0:T(256)S(1)} %select_reduce_fusion), channel_id=1, replica_groups=mesh['dp'=16,'expert'=2] {'dp'}, use_global_device_ids=true, to_apply=%region_16.17 | all-reduce | flops 256 | bytes 2048 | tf_op jit(solution)/shard_map/pmin | solution.py:80
  194.0 38.4 %psum.15 = f32[256]{0:T(256)S(1)} all-reduce(f32[256]{0:T(256)S(1)} %convert_element_type.90), channel_id=1, replica_groups=mesh['dp'=16,'expert'=2] {'dp'}, use_global_device_ids=true, to_apply=%region_19.20 | all-reduce | flops 256 | bytes 2048 | tf_op jit(solution)/shard_map/psum | solution.py:85
  232.4 1.3 fusion.20
  233.7 0.6 select_convert_fusion
  234.2 45.3 %all-reduce.2.cloned.1.call-done = f32[256,4096]{1,0:T(8,128)} async-done(((f32[256,4096]{1,0:T(8,128)}), f32[256,4096]{1,0:T(8,128)}) %all-reduce.2.cloned.1.call-update) | async-done | bytes 4194320 | tf_op jit(solution)/shard_map/psum | solution.py:85
  279.5 5.1 %add_convert_fusion = bf16[256,4096]{1,0:T(8,128)(2,1)} fusion(f32[256,4096]{1,0:T(8,128)} %all-reduce.2.cloned.1.call-done, bf16[256,4096]{1,0:T(8,128)(2,1)} %param.5, f32[256]{0:T(256)S(1)} %broadcast_maximum_fusion), kind=kLoop, calls=%fused_computation | loop fusion | flops 6291456 | bytes 8389632 | tf_op jit(solution)/shard_map/convert_element_type | solution.py:88
  (24 shorter events, 0.2 us)
Async XLA Ops:
  7.2 1.9 copy-start
  7.2 4.8 %copy-start.3 = (f32[256]{0:T(256)S(1)}, f32[256]{0:T(256)}, u32[]{:S(2)}) copy-start(f32[256]{0:T(256)} %param.6) | copy-start | bytes 3076
  7.2 272.3 %all-reduce.2.cloned.1.call-start = ((), (), s32[]{:S(2)}) async-start(), calls=%async_computation | async-start | bytes 8388608 | tf_op jit(solution)/shard_map/psum | solution.py:85
  104.6 2.1 copy-start.1
  104.9 3.6 %copy-start.2 = (s32[384]{0:T(512)}, s32[384]{0:T(512)S(1)}, u32[]{:S(2)}) copy-start(s32[384]{0:T(512)S(1)} %select_reduce_fusion.2) | copy-start | bytes 4612
Sparse Core Ops, SparseCore 0:
  112.5 167.0 all-reduce.1
where the time goes:
time: 292 us; the launch traced here: 291 us
  blocking collectives  212 us (73%)
  waiting for transfers between devices  45.3 us (16%)
  between operations  14.8 us (5%)
  other arithmetic  11.2 us (4%)
  matrix products  6.14 us (2%)
    pmax x3, blocking collectives, body(): top_bid = lax.pmax(local_bid, 'dp')  120 us
    psum x1, waiting for transfers between devices, body(): feature_sums, counts = lax.psum((local_sums, local_counts), 'dp')  45.3 us
    psum x1, blocking collectives, body(): feature_sums, counts = lax.psum((local_sums, local_counts), 'dp')  38.4 us
    pmin x1, blocking collectives, body(): first_float = lax.pmin(local_first, 'dp')  37.2 us
    all_gather x9, blocking collectives, merged(): pieces = jax.tree.map(lambda part: lax.all_gather(part, axis), value)  16.1 us
  transfers between devices with their start and end apart: 1, of which 1 were waited for; matrix products, arithmetic and copies ran while one was open for 1% of the time, Pallas kernels for 0%

commit v1 on v0

v1 whole, which is shorter than its diff:
```python
import functools

import jax
import jax.numpy as jnp
from jax import lax
from jax.experimental import pallas as pl
from jax.experimental.pallas import tpu as pltpu
from jax.sharding import PartitionSpec as P

ROUNDS = 3

lowest = -1e30
far = 1073741824.0
VMEM = pl.BlockSpec(memory_space=pltpu.VMEM)
SMEM = pl.BlockSpec(memory_space=pltpu.SMEM)
ANY = pl.BlockSpec(memory_space=pl.ANY)


def choose(scores, current, eps):
    values = scores - current
    ids = lax.broadcasted_iota(jnp.int32, values.shape, 1).astype(jnp.float32)
    top = jnp.max(values, axis=1, keepdims=True)
    choice = jnp.min(jnp.where(values == top, ids, far), axis=1, keepdims=True)
    claims = ids == choice
    second = jnp.max(jnp.where(claims, lowest, values), axis=1, keepdims=True)
    bid = top - second + eps
    bids = jnp.where(claims, bid, -1.0)
    return choice, claims, bid, bids, jnp.max(bids, axis=0, keepdims=True)


def first_round(scores, prices, epsilon, out):
    raised = choose(scores[...], prices[...], epsilon[0])[4]
    out[...] = jnp.broadcast_to(raised[None], out.shape)


def next_round(scores, prices, epsilon, bids, out, new_prices):
    top_bid = jnp.max(bids[...], axis=0)
    current = prices[...] + jnp.maximum(top_bid, 0.0)
    new_prices[...] = current
    raised = choose(scores[...], current, epsilon[0])[4]
    out[...] = jnp.broadcast_to(raised[None], out.shape)


def last_round(scores, prices, epsilon, bids, base, out, new_prices):
    experts = prices.shape[1]
    rows = scores.shape[0]
    top_bid = jnp.max(bids[...], axis=0)
    current = prices[...] + jnp.maximum(top_bid, 0.0)
    new_prices[...] = current
    choice, claims, bid, spread, raised = choose(scores[...], current, epsilon[0])
    token = (base[0] + lax.broadcasted_iota(jnp.int32, (rows, experts), 0)).astype(jnp.float32)
    first = jnp.min(jnp.where(claims & (spread == raised), token, far), axis=0, keepdims=True)
    count = jnp.sum(claims.astype(jnp.float32), axis=0, keepdims=True)
    wide = out.shape[2] - 3 * experts
    lane = lax.broadcasted_iota(jnp.int32, (rows, wide), 1)
    row = lax.broadcasted_iota(jnp.int32, (rows, wide), 0)
    turned = jnp.sum(jnp.where(lane == row, choice, 0.0), axis=0, keepdims=True)
    line = jnp.concatenate([raised, first, count, turned], axis=1)
    out[...] = jnp.broadcast_to(line[None], out.shape)


def finish(rows, swap, info, place, prices, centroids, *refs):
    columns, (final, holder, block) = refs[:-3], refs[-3:]
    devices = info.shape[0]
    experts = prices.shape[1]
    own = centroids.shape[0]
    raised = info[:, :, :experts]
    top_bid = jnp.max(raised, axis=0)
    final[...] = prices[...] + jnp.maximum(top_bid, 0.0)
    firsts = jnp.where(raised == top_bid[None], info[:, :, experts : 2 * experts], far)
    first = jnp.min(firsts, axis=0)
    holder[...] = jnp.where(top_bid > 0, first, -1.0).astype(jnp.int32)
    counts = jnp.sum(info[:, :, 2 * experts : 3 * experts], axis=0)
    ids = (place[0] + lax.broadcasted_iota(jnp.int32, (own, rows), 0)).astype(jnp.float32)
    total = jnp.zeros((own, sum(c.shape[2] for c in columns)), jnp.float32)
    for n in range(devices):
        hot = jnp.where(ids == info[n, :, 3 * experts : 3 * experts + rows], 1.0, 0.0)
        features = [c[n] for c in columns]
        features = features[0] if len(features) == 1 else jnp.concatenate(features, axis=1)
        total += jnp.dot(
            hot.astype(jnp.bfloat16), features, preferred_element_type=jnp.float32
        )
    if swap:
        half = total.shape[1] // 2
        left, right = total[:, :half], total[:, half:]
        total = jnp.concatenate(
            [jnp.where(place[2] == 0, left, right), jnp.where(place[2] == 0, right, left)], axis=1
        )
    expert_row = (place[0] + lax.broadcasted_iota(jnp.int32, (own, experts), 0))
    lane = lax.broadcasted_iota(jnp.int32, (own, experts), 1)
    mine = jnp.sum(jnp.where(expert_row == lane, counts, 0.0), axis=1, keepdims=True)
    fresh = 0.5 * centroids[...].astype(jnp.float32) + 0.5 * total / jnp.maximum(mine, 1.0)
    fresh = fresh.astype(jnp.bfloat16)
    half = own // 2
    block[0] = fresh[:half]
    block[1] = fresh[half:]


def assemble(plan, base, *refs):
    pieces, out, sem = refs[:-2], refs[-2], refs[-1]
    half, cols = pieces[0].shape[1:]
    copies = []
    for piece, slots in zip(pieces, plan):
        for i, (part, slot) in enumerate(slots):
            col = pl.multiple_of(base[slot] * cols, cols)
            copies.append(
                pltpu.make_async_copy(
                    piece.at[i], out.at[pl.ds(part * half, half), pl.ds(col, cols)], sem.at[len(copies)]
                )
            )
    for copy in copies:
        copy.start()
    for copy in copies:
        copy.wait()


def gather_columns(block, n):
    if n % 4 or block.shape[2] % 128:
        return lax.all_gather(block.reshape(-1, block.shape[2]), "dp", axis=1, tiled=True)
    line = n // 4
    me = lax.axis_index("dp")

    def move(value, step, flip):
        def to(i):
            return (i // 4 + step) % line * 4 + (i % 4 ^ flip)

        return lax.ppermute(value, "dp", [(i, to(i)) for i in range(n)])

    up, down = {0: block}, {0: block}
    got = [(block, [(0, (0, 0)), (1, (0, 0))])]
    one, two = block[0:1], block[1:2]
    near = {0: (one, two)}
    steps = (line - 1) // 2
    for s in range(1, steps + 1):
        up[s] = move(up[s - 1], 1, 0)
        down[s] = move(down[s - 1], -1, 0)
        got.append((up[s], [(0, (-s, 0)), (1, (-s, 0))]))
        got.append((down[s], [(0, (s, 0)), (1, (s, 0))]))
        near[-s] = (up[s][0:1], up[s][1:2])
        near[s] = (down[s][0:1], down[s][1:2])
    if line % 2 == 0:
        s = line // 2
        a = move(near[-(s - 1)][0], 1, 0)
        b = move(near[s - 1][1], -1, 0)
        got.append((a, [(0, (s, 0))]))
        got.append((b, [(1, (s, 0))]))
        near[s] = (a, b)

    def plane(offsets):
        ones = jnp.concatenate([near[o][0] for o in offsets]) if len(offsets) > 1 else near[offsets[0]][0]
        twos = jnp.concatenate([near[o][1] for o in offsets]) if len(offsets) > 1 else near[offsets[0]][1]
        ax, ay = move(ones, 0, 1), move(ones, 0, 2)
        bx, by = move(twos, 0, 1), move(twos, 0, 2)
        ad = move(ax, 0, 2)
        bd = move(by, 0, 1)
        for value, part, flip in ((ax, 0, 1), (ay, 0, 2), (bx, 1, 1), (by, 1, 2), (ad, 0, 3), (bd, 1, 3)):
            got.append((value, [(part, (o, flip)) for o in offsets]))

    plane([0])
    if line > 1:
        plane([o for o in near if o])
    slots = sorted({slot for _, entry in got for _, slot in entry})
    base = jnp.stack([(me // 4 + o) % line * 4 + (me % 4 ^ f) for o, f in slots]).astype(jnp.int32)
    plan = [[(part, slots.index(slot)) for part, slot in entry] for _, entry in got]
    half, cols = block.shape[1:]
    return pl.pallas_call(
        functools.partial(assemble, plan),
        out_shape=jax.ShapeDtypeStruct((2 * half, n * cols), block.dtype),
        in_specs=[SMEM] + [ANY] * len(got),
        out_specs=ANY,
        scratch_shapes=[pltpu.SemaphoreType.DMA((sum(map(len, plan)),))],
        name="assemble",
    )(base, *[value for value, _ in got])


def body(dp, ne, tokens, centroids, prices, epsilon):
    f32 = jnp.float32
    local_tokens, width = tokens.shape
    own = centroids.shape[0]
    experts = own * ne
    devices = dp * ne
    rows = local_tokens // ne
    cols = width // dp
    dp_at, expert_at = lax.axis_index("dp"), lax.axis_index("expert")
    everywhere = ("dp", "expert")

    paired = ne == 2 and (cols // 2) % 128 == 0
    if paired:
        sub = cols // 2
        mine = lax.dynamic_slice_in_dim(tokens, expert_at * rows, rows, 0)
        parcels = mine.reshape(rows, devices, sub).transpose(1, 0, 2)
        columns = lax.all_to_all(parcels, everywhere, 0, 0, tiled=True)
        columns = [columns, lax.ppermute(columns, "expert", [(0, 1), (1, 0)])]
    else:
        parcels = tokens.reshape(local_tokens, dp, cols).transpose(1, 0, 2)
        columns = lax.all_to_all(parcels, "dp", 0, 0, tiled=True)
        columns = [columns.reshape(devices, rows, cols)]

    part = lax.dot_general(
        tokens, centroids, (((1,), (1,)), ((), ())), preferred_element_type=f32
    ) * 0.015625
    if ne == 2:
        theirs = lax.dynamic_slice_in_dim(part, (1 - expert_at) * rows, rows, 0)
        kept = lax.dynamic_slice_in_dim(part, expert_at * rows, rows, 0)
        theirs = lax.ppermute(theirs, "expert", [(0, 1), (1, 0)])
        scores = jnp.concatenate(
            [jnp.where(expert_at == 0, kept, theirs), jnp.where(expert_at == 0, theirs, kept)], axis=1
        )
    else:
        scores = lax.all_to_all(part, "expert", 0, 1, tiled=True)
    current = lax.all_gather(prices, "expert", tiled=True).reshape(1, experts)

    line = jax.ShapeDtypeStruct((1, experts), f32)
    spread = jax.ShapeDtypeStruct((devices, 1, experts), f32)
    bids = pl.pallas_call(
        first_round, out_shape=spread, in_specs=[VMEM, VMEM, SMEM], out_specs=VMEM, name="first_round"
    )(scores, current, epsilon)
    for _ in range(ROUNDS - 2):
        bids = lax.all_to_all(bids, everywhere, 0, 0, tiled=True)
        bids, current = pl.pallas_call(
            next_round,
            out_shape=(spread, line),
            in_specs=[VMEM, VMEM, SMEM, VMEM],
            out_specs=(VMEM, VMEM),
            name="next_round",
        )(scores, current, epsilon, bids)
    bids = lax.all_to_all(bids, everywhere, 0, 0, tiled=True)
    wide = -(-rows // 128) * 128
    base = (dp_at * local_tokens + expert_at * rows).astype(jnp.int32).reshape(1)
    info, current = pl.pallas_call(
        last_round,
        out_shape=(jax.ShapeDtypeStruct((devices, 1, 3 * experts + wide), f32), line),
        in_specs=[VMEM, VMEM, SMEM, VMEM, SMEM],
        out_specs=(VMEM, VMEM),
        name="last_round",
    )(scores, current, epsilon, bids, base)
    info = lax.all_to_all(info, everywhere, 0, 0, tiled=True)

    place = jnp.stack([expert_at * own, dp_at, expert_at]).astype(jnp.int32)
    my_centroids = lax.dynamic_slice_in_dim(centroids, dp_at * cols, cols, 1)
    final, holder, block = pl.pallas_call(
        functools.partial(finish, rows, paired),
        out_shape=(
            line,
            jax.ShapeDtypeStruct((1, experts), jnp.int32),
            jax.ShapeDtypeStruct((2, own // 2, cols), jnp.bfloat16),
        ),
        in_specs=[VMEM, SMEM, VMEM, VMEM] + [VMEM] * len(columns),
        out_specs=(VMEM, VMEM, VMEM),
        name="finish",
        compiler_params=pltpu.CompilerParams(vmem_limit_bytes=40 * 1024 * 1024),
    )(info, place, current, my_centroids, *columns)
    refreshed = gather_columns(block, dp)
    best = lax.dynamic_slice_in_dim(info, dp_at * ne, ne, 0)[:, 0, 3 * experts : 3 * experts + rows]
    best = best.reshape(local_tokens).astype(jnp.int32)
    final = lax.dynamic_slice_in_dim(final[0], expert_at * own, own, 0)
    holder = lax.dynamic_slice_in_dim(holder[0], expert_at * own, own, 0)
    return final, best, holder, refreshed


def solution(mesh):
    placed = (P("dp", None), P("expert", None), P("expert"), P())
    return jax.shard_map(
        functools.partial(body, mesh.shape["dp"], mesh.shape["expert"]),
        mesh=mesh,
        in_specs=placed,
        out_specs=(P("expert"), P("dp"), P("expert"), P("expert", None)),
        check_vma=False,
    )
```

time: 292 us -> 204 us (0.70)
  blocking collectives: 212 us -> 57.8 us
  Pallas kernels: 0 us -> 74.7 us
  starting transfers between devices: 0.04 us -> 24.8 us
  waiting for transfers between devices: 45.3 us -> 27.9 us
  between operations: 14.8 us -> 1.46 us
  local copies, waits for them, and re-layouts: 1.89 us -> 12.5 us
  other arithmetic: 11.2 us -> 3.26 us
  matrix products: 6.14 us -> 1.03 us
    pmax x3 -> x0, blocking collectives: 120 us -> none  [body(): top_bid = lax.pmax(local_bid, 'dp')]
    pallas_call x0 -> x5, Pallas kernels: none -> 74.7 us  [the longest x1 65.6 us: gather_columns(): pl.pallas_call(functools.partial(assemble, plan), out_shape=jax.ShapeDtyp...]
    all_to_all x0 -> x2, blocking collectives: none -> 55.9 us  [the longest x1 45.2 us: body(): columns = lax.all_to_all(parcels, everywhere, 0, 0, tiled=True)]
    psum x1 -> x0, waiting for transfers between devices: 45.3 us -> none  [body(): feature_sums, counts = lax.psum((local_sums, local_counts), 'dp')]
    psum x1 -> x0, blocking collectives: 38.4 us -> none  [body(): feature_sums, counts = lax.psum((local_sums, local_counts), 'dp')]
    pmin x1 -> x0, blocking collectives: 37.2 us -> none  [body(): first_float = lax.pmin(local_first, 'dp')]
    ppermute x0 -> x18, starting transfers between devices: none -> 19.6 us  [the longest x16 19.1 us: move(): return lax.ppermute(value, 'dp', [(i, to(i)) for i in range(n)])]
    all_to_all x0 -> x2, waiting for transfers between devices: none -> 15.6 us  [the longest x1 8.17 us: body(): info = lax.all_to_all(info, everywhere, 0, 0, tiled=True)]
  transfers between devices with their start and end apart: 1 -> 20, of which waited for: 1 -> 8; matrix products, arithmetic and copies ran while one was open for 1% -> 5% of each run, Pallas kernels for 0% -> 3%
where the time goes in v1:
time: 204 us
  Pallas kernels  74.7 us (37%)
  blocking collectives  57.8 us (28%)
  waiting for transfers between devices  27.9 us (14%)
  starting transfers between devices  24.8 us (12%)
  local copies, waits for them, and re-layouts  12.5 us (6%)
  other arithmetic  3.26 us (2%)
    pallas_call x1, Pallas kernels, gather_columns(): pl.pallas_call(functools.partial(assemble, plan), out_shape=jax.ShapeDtyp...  65.6 us
    all_to_all x1, blocking collectives, body(): columns = lax.all_to_all(parcels, everywhere, 0, 0, tiled=True)  45.2 us
    ppermute x16, starting transfers between devices, move(): return lax.ppermute(value, 'dp', [(i, to(i)) for i in range(n)])  19.1 us
    ppermute x16, waiting for transfers between devices, move(): return lax.ppermute(value, 'dp', [(i, to(i)) for i in range(n)])  12.3 us
    all_to_all x1, blocking collectives, body(): bids = lax.all_to_all(bids, everywhere, 0, 0, tiled=True)  10.7 us
    all_to_all x1, waiting for transfers between devices, body(): info = lax.all_to_all(info, everywhere, 0, 0, tiled=True)  8.17 us
    all_to_all x1, waiting for transfers between devices, body(): bids = lax.all_to_all(bids, everywhere, 0, 0, tiled=True)  7.4 us
    unnamed x28, local copies, waits for them, and re-layouts  6.76 us
  transfers between devices with their start and end apart: 20, of which 8 were waited for; matrix products, arithmetic and copies ran while one was open for 5% of the time, Pallas kernels for 3%

profile of v1, /device:TPU:0, one launch (start us, length us, event | category | flops | bytes accessed | tf_op | source)
XLA Modules:
  0.0 203.5 jit_solution(5640918494007077566)
XLA Ops:
  0.7 1.9 copy-done
  3.0 45.2 %all_to_all.20.refs_0_ = bf16[32,192,128]{2,1,0:T(8,128)(2,1)} all-to-all(bf16[32,192,128]{2,1,0:T(8,128)(2,1)S(1)} %bitcast_bitcast_fusion), channel_id=1, replica_groups=mesh['dp'=16,'expert'=2] {'dp','expert'}, dimensions={0} | all-to-all | bytes 3145728 | tf_op jit(solution)/shard_map/all_to_all | solution.py:192
  48.2 1.0 convolution_multiply_fusion
  49.2 0.7 constant_dynamic-slice_fusion.3
  51.1 1.9 all-gather
  53.0 1.0 dynamic-slice_select_fusion.1
  54.0 0.8 pad_maximum_fusion.scores
  54.8 1.9 first_round.1
  56.7 10.7 %all_to_all.21.bids = f32[32,1,512]{2,1,0:T(1,128)} all-to-all(f32[32,1,512]{2,1,0:T(1,128)} %first_round.1), channel_id=1, replica_groups=mesh['dp'=16,'expert'=2] {'dp','expert'}, dimensions={0} | all-to-all | bytes 131072 | tf_op jit(solution)/shard_map/all_to_all | solution.py:219
  67.3 1.9 next_round.1
  69.3 2.6 %all-to-all-start.1 = ((f32[32,1,512]{2,1,0:T(1,128)}), f32[32,1,512]{2,1,0:T(1,128)S(1)}, u32[]{:S(2)}, u32[]{:S(2)}) async-start(f32[32,1,512]{2,1,0:T(1,128)} %get-tuple-element.12), calls=%async_computation.1 | async-start | bytes 131072 | tf_op jit(solution)/shard_map/all_to_all | solution.py:227
  71.9 7.4 %all-to-all-done.1.bids = f32[32,1,512]{2,1,0:T(1,128)S(1)} async-done(((f32[32,1,512]{2,1,0:T(1,128)}), f32[32,1,512]{2,1,0:T(1,128)S(1)}, u32[]{:S(2)}, u32[]{:S(2)}) %all-to-all-start.1) | async-done | bytes 65568 | tf_op jit(solution)/shard_map/all_to_all | solution.py:227
  79.3 0.6 copy-done.8
  79.9 2.1 %last_round.1 = (f32[32,1,1792]{2,1,0:T(1,128)}, f32[1,512]{1,0:T(1,128)}) custom-call(f32[192,512]{1,0:T(8,128)} %pad_maximum_fusion.scores, f32[1,512]{1,0:T(1,128)} %get-tuple-element.11.prices, f32[1]{0:T(128)S(6)} %copy.12.epsilon, f32[32,1,512]{2,1,0:T(1,128)} %copy-done.8, s32[1]{0:T(128)} %bitcast.2.base), custom_call_target="tpu_custom_call" | custom-call | tf_op jit(solution)/shard_map/last_round/pallas_call | solution.py:230
  82.0 2.6 %all-to-all-start.2 = ((f32[32,1,1792]{2,1,0:T(1,128)}), f32[32,1,1792]{2,1,0:T(1,128)S(1)}, u32[]{:S(2)}, u32[]{:S(2)}) async-start(f32[32,1,1792]{2,1,0:T(1,128)} %get-tuple-element.13), calls=%async_computation.2 | async-start | bytes 458752 | tf_op jit(solution)/shard_map/all_to_all | solution.py:237
  84.7 1.6 constant_dynamic-slice_fusion.2.centroids
  86.2 8.2 %all-to-all-done.2.info = f32[32,1,1792]{2,1,0:T(1,128)S(1)} async-done(((f32[32,1,1792]{2,1,0:T(1,128)}), f32[32,1,1792]{2,1,0:T(1,128)S(1)}, u32[]{:S(2)}, u32[]{:S(2)}) %all-to-all-start.2) | async-done | bytes 229408 | tf_op jit(solution)/shard_map/all_to_all | solution.py:237
  94.4 0.9 copy-done.2
  95.3 0.7 copy-done.3
  96.0 3.2 %finish.1 = (f32[1,512]{1,0:T(1,128)S(1)}, s32[1,512]{1,0:T(1,128)S(1)}, bf16[2,128,256]{2,1,0:T(8,128)(2,1)S(1)}) custom-call(f32[32,1,1792]{2,1,0:T(1,128)S(1)} %all-to-all-done.2.info, s32[3]{0:T(128)S(1)} %pad_add_fusion.place, f32[1,512]{1,0:T(1,128)S(1)} %copy-done.3, bf16[256,256]{1,0:T(8,128)(2,1)S(1)} %copy-done.2, ...), custom_call_target="tpu_custom_call" | custom-call | tf_op jit(solution)/shard_map/finish/pallas_call | solution.py:241
  99.2 1.1 collective-permute-start.2
  100.3 2.8 %collective-permute-start.3 = (bf16[2,128,256]{2,1,0:T(8,128)(2,1)S(1)}, bf16[2,128,256]{2,1,0:T(8,128)(2,1)S(1)}, u32[]{:S(2)}, u32[]{:S(2)}) collective-permute-start(bf16[2,128,256]{2,1,0:T(8,128)(2,1)S(1)} %get-tuple-element.17.refs_0_), channel_id=1, source_target_pairs={{0,24},{2,26},{4,28},{6,30},{8,0},{10,2},{12,4},{14,6},{16,8},{18,... | collective-permute-start | bytes 393224 | tf_op jit(solution)/shard_map/ppermute | solution.py:127
  103.1 4.4 %collective-permute-done.2.refs_1_ = bf16[2,128,256]{2,1,0:T(8,128)(2,1)S(1)} collective-permute-done((bf16[2,128,256]{2,1,0:T(8,128)(2,1)S(1)}, bf16[2,128,256]{2,1,0:T(8,128)(2,1)S(1)}, u32[]{:S(2)}, u32[]{:S(2)}) %collective-permute-start.2) | collective-permute-done | bytes 131104 | tf_op jit(solution)/shard_map/ppermute | solution.py:127
  108.2 0.6 copy-done.5
  108.8 3.2 %collective-permute-start.5 = (bf16[1,128,256]{2,1,0:T(8,128)(2,1)S(1)}, bf16[1,128,256]{2,1,0:T(8,128)(2,1)S(1)}, u32[]{:S(2)}, u32[]{:S(2)}) collective-permute-start(bf16[1,128,256]{2,1,0:T(8,128)(2,1)S(1)} %get-tuple-element.23), channel_id=1, source_target_pairs={{0,24},{2,26},{4,28},{6,30},{8,0},{10,2},{12,4},{14,6},{16,8},{18,... | collective-permute-start | bytes 196616 | tf_op jit(solution)/shard_map/ppermute | solution.py:127
  112.0 1.7 collective-permute-done.4.refs_3_
  113.8 0.6 copy-done.6
  114.4 0.7 pad_maximum_fusion.1
  115.1 0.8 collective-permute-start.12
  116.5 0.7 pad_maximum_fusion.2
  117.2 1.0 collective-permute-start.15
  118.2 0.7 fusion.3
  118.8 1.0 collective-permute-start.9
  119.9 1.3 collective-permute-start.8
  121.1 0.8 collective-permute-start.7
  122.0 1.9 collective-permute-done.9.refs_8_
  123.9 1.3 collective-permute-start.6
  125.1 0.6 stack.83.base
  125.8 0.7 convert_element_type.7
  126.5 0.8 collective-permute-start.11
  127.2 1.0 collective-permute-start.13
  128.2 0.9 collective-permute-done.6.refs_5_
  129.2 1.2 collective-permute-start.14
  130.4 0.8 collective-permute-start.16
  131.2 0.9 collective-permute-start.17
  132.7 1.1 collective-permute-start.10
  134.4 2.9 %collective-permute-done.10.refs_9_ = bf16[1,128,256]{2,1,0:T(8,128)(2,1)S(1)} collective-permute-done((bf16[1,128,256]{2,1,0:T(8,128)(2,1)}, bf16[1,128,256]{2,1,0:T(8,128)(2,1)S(1)}, u32[]{:S(2)}, u32[]{:S(2)}) %collective-permute-start.10) | collective-permute-done | bytes 65568 | tf_op jit(solution)/shard_map/ppermute | solution.py:127
  137.9 65.6 %assemble.1 = bf16[256,4096]{1,0:T(8,128)(2,1)} custom-call(s32[16]{0:T(128)} %stack.83.base, bf16[2,128,256]{2,1,0:T(8,128)(2,1)} %copy-done.1, bf16[2,128,256]{2,1,0:T(8,128)(2,1)} %copy-done.4, bf16[2,128,256]{2,1,0:T(8,128)(2,1)} %copy-done.5, bf16[1,128,256]{2,1,0:T(8,128)(2,1)} %copy-done.6, bf16[1,128,256]{2,1,0:T(8,128)(2,1)} %copy-done.7, ...), custom_call_target="tpu_custom_call" | custom-call | tf_op jit(solution)/shard_map/assemble/pallas_call | solution.py:166
  (45 shorter events, 4.2 us)
Async XLA Ops:
  0.6 1.9 copy-start
  3.0 45.2 %copy-start.12 = (bf16[256,4096]{1,0:T(8,128)(2,1)S(1)}, bf16[256,4096]{1,0:T(8,128)(2,1)}, u32[]{:S(2)}) copy-start(bf16[256,4096]{1,0:T(8,128)(2,1)} %param.5) | copy-start | bytes 6291460
  48.2 2.9 %copy-start.13 = (f32[256]{0:T(256)S(1)}, f32[256]{0:T(256)}, u32[]{:S(2)}) copy-start(f32[256]{0:T(256)} %param.6) | copy-start | bytes 3076
  48.2 46.2 %collective-permute-start.1 = (bf16[32,192,128]{2,1,0:T(8,128)(2,1)}, bf16[32,192,128]{2,1,0:T(8,128)(2,1)}, u32[]{:S(2)}, u32[]{:S(2)}) collective-permute-start(bf16[32,192,128]{2,1,0:T(8,128)(2,1)} %all_to_all.20.refs_0_), channel_id=1, source_target_pairs={{0,1},{1,0},{2,3},{3,2},{4,5},{5,4},{6,7},{7,6},{8,9},{9,8},{10,11... | collective-permute-start | bytes 4718600 | tf_op jit(solution)/shard_map/ppermute | solution.py:193
  49.9 3.1 %collective-permute-start = (f32[192,256]{1,0:T(8,128)}, f32[192,256]{1,0:T(8,128)}, u32[]{:S(2)}, u32[]{:S(2)}) collective-permute-start(f32[192,256]{1,0:T(8,128)} %constant_dynamic-slice_fusion.3), channel_id=1, source_target_pairs={{0,1},{1,0},{2,3},{3,2},{4,5},{5,4},{6,7},{7,6},{8,9},{9,8},{10,11... | collective-permute-start | bytes 589832 | tf_op jit(solution)/shard_map/ppermute | solution.py:205
  69.3 10.0 %all-to-all-start.1 = ((f32[32,1,512]{2,1,0:T(1,128)}), f32[32,1,512]{2,1,0:T(1,128)S(1)}, u32[]{:S(2)}, u32[]{:S(2)}) async-start(f32[32,1,512]{2,1,0:T(1,128)} %get-tuple-element.12), calls=%async_computation.1 | async-start | bytes 131072 | tf_op jit(solution)/shard_map/all_to_all | solution.py:227
  79.3 0.6 copy-start.8
  82.0 12.4 %all-to-all-start.2 = ((f32[32,1,1792]{2,1,0:T(1,128)}), f32[32,1,1792]{2,1,0:T(1,128)S(1)}, u32[]{:S(2)}, u32[]{:S(2)}) async-start(f32[32,1,1792]{2,1,0:T(1,128)} %get-tuple-element.13), calls=%async_computation.2 | async-start | bytes 458752 | tf_op jit(solution)/shard_map/all_to_all | solution.py:237
  94.4 0.9 copy-start.2
  95.3 0.7 copy-start.3
  99.2 38.6 %copy-start.1 = (bf16[2,128,256]{2,1,0:T(8,128)(2,1)}, bf16[2,128,256]{2,1,0:T(8,128)(2,1)S(1)}, u32[]{:S(2)}) copy-start(bf16[2,128,256]{2,1,0:T(8,128)(2,1)S(1)} %get-tuple-element.17.refs_0_) | copy-start | bytes 393220
  99.2 8.3 %collective-permute-start.2 = (bf16[2,128,256]{2,1,0:T(8,128)(2,1)S(1)}, bf16[2,128,256]{2,1,0:T(8,128)(2,1)S(1)}, u32[]{:S(2)}, u32[]{:S(2)}) collective-permute-start(bf16[2,128,256]{2,1,0:T(8,128)(2,1)S(1)} %get-tuple-element.17.refs_0_), channel_id=1, source_target_pairs={{0,8},{2,10},{4,12},{6,14},{8,16},{10,18},{12,20},{14,22},{16,24},... | collective-permute-start | bytes 393224 | tf_op jit(solution)/shard_map/ppermute | solution.py:127
  100.3 7.8 %collective-permute-start.3 = (bf16[2,128,256]{2,1,0:T(8,128)(2,1)S(1)}, bf16[2,128,256]{2,1,0:T(8,128)(2,1)S(1)}, u32[]{:S(2)}, u32[]{:S(2)}) collective-permute-start(bf16[2,128,256]{2,1,0:T(8,128)(2,1)S(1)} %get-tuple-element.17.refs_0_), channel_id=1, source_target_pairs={{0,24},{2,26},{4,28},{6,30},{8,0},{10,2},{12,4},{14,6},{16,8},{18,... | collective-permute-start | bytes 393224 | tf_op jit(solution)/shard_map/ppermute | solution.py:127
  107.5 0.7 copy-start.4
  107.5 6.2 %collective-permute-start.4 = (bf16[1,128,256]{2,1,0:T(8,128)(2,1)S(1)}, bf16[1,128,256]{2,1,0:T(8,128)(2,1)S(1)}, u32[]{:S(2)}, u32[]{:S(2)}) collective-permute-start(bf16[1,128,256]{2,1,0:T(8,128)(2,1)S(1)} %get-tuple-element.21), channel_id=1, source_target_pairs={{0,8},{2,10},{4,12},{6,14},{8,16},{10,18},{12,20},{14,22},{16,24},... | collective-permute-start | bytes 196616 | tf_op jit(solution)/shard_map/ppermute | solution.py:127
  108.1 0.6 copy-start.5
  108.8 7.0 %collective-permute-start.5 = (bf16[1,128,256]{2,1,0:T(8,128)(2,1)S(1)}, bf16[1,128,256]{2,1,0:T(8,128)(2,1)S(1)}, u32[]{:S(2)}, u32[]{:S(2)}) collective-permute-start(bf16[1,128,256]{2,1,0:T(8,128)(2,1)S(1)} %get-tuple-element.23), channel_id=1, source_target_pairs={{0,24},{2,26},{4,28},{6,30},{8,0},{10,2},{12,4},{14,6},{16,8},{18,... | collective-permute-start | bytes 196616 | tf_op jit(solution)/shard_map/ppermute | solution.py:127
  113.8 0.6 copy-start.6
  115.1 15.3 %collective-permute-start.12 = (bf16[3,128,256]{2,1,0:T(8,128)(2,1)}, bf16[3,128,256]{2,1,0:T(8,128)(2,1)}, u32[]{:S(2)}, u32[]{:S(2)}) collective-permute-start(bf16[3,128,256]{2,1,0:T(8,128)(2,1)} %pad_maximum_fusion.1), channel_id=1, source_target_pairs={{0,2},{2,0},{4,6},{6,4},{8,10},{10,8},{12,14},{14,12},{16,18},{18,... | collective-permute-start | bytes 589832 | tf_op jit(solution)/shard_map/ppermute | solution.py:127
  115.8 0.6 copy-start.7
  117.2 14.1 %collective-permute-start.15 = (bf16[3,128,256]{2,1,0:T(8,128)(2,1)}, bf16[3,128,256]{2,1,0:T(8,128)(2,1)}, u32[]{:S(2)}, u32[]{:S(2)}) collective-permute-start(bf16[3,128,256]{2,1,0:T(8,128)(2,1)} %pad_maximum_fusion.2), channel_id=1, source_target_pairs={{0,4},{2,6},{4,0},{6,2},{8,12},{10,14},{12,8},{14,10},{16,20},{18,... | collective-permute-start | bytes 589832 | tf_op jit(solution)/shard_map/ppermute | solution.py:127
  118.8 5.0 %collective-permute-start.9 = (bf16[1,128,256]{2,1,0:T(8,128)(2,1)}, bf16[1,128,256]{2,1,0:T(8,128)(2,1)}, u32[]{:S(2)}, u32[]{:S(2)}) collective-permute-start(bf16[1,128,256]{2,1,0:T(8,128)(2,1)} %get-tuple-element.24), channel_id=1, source_target_pairs={{0,4},{2,6},{4,0},{6,2},{8,12},{10,14},{12,8},{14,10},{16,20},{18,... | collective-permute-start | bytes 196616 | tf_op jit(solution)/shard_map/ppermute | solution.py:127
  119.9 6.6 %collective-permute-start.8 = (bf16[1,128,256]{2,1,0:T(8,128)(2,1)}, bf16[1,128,256]{2,1,0:T(8,128)(2,1)}, u32[]{:S(2)}, u32[]{:S(2)}) collective-permute-start(bf16[1,128,256]{2,1,0:T(8,128)(2,1)} %get-tuple-element.24), channel_id=1, source_target_pairs={{0,2},{2,0},{4,6},{6,4},{8,10},{10,8},{12,14},{14,12},{16,18},{18,... | collective-permute-start | bytes 196616 | tf_op jit(solution)/shard_map/ppermute | solution.py:127
  121.1 6.1 %collective-permute-start.7 = (bf16[1,128,256]{2,1,0:T(8,128)(2,1)}, bf16[1,128,256]{2,1,0:T(8,128)(2,1)}, u32[]{:S(2)}, u32[]{:S(2)}) collective-permute-start(bf16[1,128,256]{2,1,0:T(8,128)(2,1)} %get-tuple-element.25), channel_id=1, source_target_pairs={{0,4},{2,6},{4,0},{6,2},{8,12},{10,14},{12,8},{14,10},{16,20},{18,... | collective-permute-start | bytes 196616 | tf_op jit(solution)/shard_map/ppermute | solution.py:127
  123.9 5.3 %collective-permute-start.6 = (bf16[1,128,256]{2,1,0:T(8,128)(2,1)}, bf16[1,128,256]{2,1,0:T(8,128)(2,1)}, u32[]{:S(2)}, u32[]{:S(2)}) collective-permute-start(bf16[1,128,256]{2,1,0:T(8,128)(2,1)} %get-tuple-element.25), channel_id=1, source_target_pairs={{0,2},{2,0},{4,6},{6,4},{8,10},{10,8},{12,14},{14,12},{16,18},{18,... | collective-permute-start | bytes 196616 | tf_op jit(solution)/shard_map/ppermute | solution.py:127
  126.5 6.3 %collective-permute-start.11 = (bf16[1,128,256]{2,1,0:T(8,128)(2,1)}, bf16[1,128,256]{2,1,0:T(8,128)(2,1)S(1)}, u32[]{:S(2)}, u32[]{:S(2)}) collective-permute-start(bf16[1,128,256]{2,1,0:T(8,128)(2,1)} %collective-permute-done.9.refs_8_), channel_id=1, source_target_pairs={{0,2},{2,0},{4,6},{6,4},{8,10},{10,8},{12,14},{14,12},{16,18},{18,... | collective-permute-start | bytes 196616 | tf_op jit(solution)/shard_map/ppermute | solution.py:127
  127.2 10.0 %collective-permute-start.13 = (bf16[3,128,256]{2,1,0:T(8,128)(2,1)}, bf16[3,128,256]{2,1,0:T(8,128)(2,1)S(1)}, u32[]{:S(2)}, u32[]{:S(2)}) collective-permute-start(bf16[3,128,256]{2,1,0:T(8,128)(2,1)} %pad_maximum_fusion.1), channel_id=1, source_target_pairs={{0,4},{2,6},{4,0},{6,2},{8,12},{10,14},{12,8},{14,10},{16,20},{18,... | collective-permute-start | bytes 589832 | tf_op jit(solution)/shard_map/ppermute | solution.py:127
  129.2 8.1 %collective-permute-start.14 = (bf16[3,128,256]{2,1,0:T(8,128)(2,1)}, bf16[3,128,256]{2,1,0:T(8,128)(2,1)}, u32[]{:S(2)}, u32[]{:S(2)}) collective-permute-start(bf16[3,128,256]{2,1,0:T(8,128)(2,1)} %pad_maximum_fusion.2), channel_id=1, source_target_pairs={{0,2},{2,0},{4,6},{6,4},{8,10},{10,8},{12,14},{14,12},{16,18},{18,... | collective-permute-start | bytes 589832 | tf_op jit(solution)/shard_map/ppermute | solution.py:127
  130.4 7.4 %collective-permute-start.16 = (bf16[3,128,256]{2,1,0:T(8,128)(2,1)}, bf16[3,128,256]{2,1,0:T(8,128)(2,1)}, u32[]{:S(2)}, u32[]{:S(2)}) collective-permute-start(bf16[3,128,256]{2,1,0:T(8,128)(2,1)} %collective-permute-done.12.refs_11_), channel_id=1, source_target_pairs={{0,4},{2,6},{4,0},{6,2},{8,12},{10,14},{12,8},{14,10},{16,20},{18,... | collective-permute-start | bytes 589832 | tf_op jit(solution)/shard_map/ppermute | solution.py:127
  131.2 6.6 %collective-permute-start.17 = (bf16[3,128,256]{2,1,0:T(8,128)(2,1)}, bf16[3,128,256]{2,1,0:T(8,128)(2,1)}, u32[]{:S(2)}, u32[]{:S(2)}) collective-permute-start(bf16[3,128,256]{2,1,0:T(8,128)(2,1)} %collective-permute-done.15.refs_14_), channel_id=1, source_target_pairs={{0,2},{2,0},{4,6},{6,4},{8,10},{10,8},{12,14},{14,12},{16,18},{18,... | collective-permute-start | bytes 589832 | tf_op jit(solution)/shard_map/ppermute | solution.py:127
  132.7 4.5 %copy-start.10 = (bf16[1,128,256]{2,1,0:T(8,128)(2,1)}, bf16[1,128,256]{2,1,0:T(8,128)(2,1)S(1)}, u32[]{:S(2)}) copy-start(bf16[1,128,256]{2,1,0:T(8,128)(2,1)S(1)} %collective-permute-done.11.refs_10_) | copy-start | bytes 196612
  132.7 4.5 %collective-permute-start.10 = (bf16[1,128,256]{2,1,0:T(8,128)(2,1)}, bf16[1,128,256]{2,1,0:T(8,128)(2,1)S(1)}, u32[]{:S(2)}, u32[]{:S(2)}) collective-permute-start(bf16[1,128,256]{2,1,0:T(8,128)(2,1)} %collective-permute-done.6.refs_5_), channel_id=1, source_target_pairs={{0,4},{2,6},{4,0},{6,2},{8,12},{10,14},{12,8},{14,10},{16,20},{18,... | collective-permute-start | bytes 196616 | tf_op jit(solution)/shard_map/ppermute | solution.py:127
  137.2 0.6 copy-start.11
  137.2 0.7 copy-start.9

commit v2 on v1

v2 whole, which is shorter than its diff:
```python
import functools

import jax
import jax.numpy as jnp
from jax import lax
from jax.experimental import pallas as pl
from jax.experimental.pallas import tpu as pltpu
from jax.sharding import PartitionSpec as P

ROUNDS = 3

lowest = -1e30
far = 1073741824.0
VMEM = pl.BlockSpec(memory_space=pltpu.VMEM)
SMEM = pl.BlockSpec(memory_space=pltpu.SMEM)
ANY = pl.BlockSpec(memory_space=pl.ANY)
ROOM = pltpu.CompilerParams(vmem_limit_bytes=32 * 1024 * 1024)


def scored(tokens, centroids, prices):
    scores = lax.dot_general(
        tokens, centroids, (((1,), (1,)), ((), ())), preferred_element_type=jnp.float32
    )
    return scores * 0.015625 - prices


def opening(place, tokens, centroids, prices, kept, sent, mine, *parcels):
    rows, cols = kept.shape[0], mine.shape[1]
    for out, at in ((sent, 1), (kept, 0)):
        row = pl.multiple_of(place[at] * rows, rows)
        out[...] = scored(tokens[pl.ds(row, rows), :], centroids[...], prices[...])
    mine[...] = centroids[:, pl.ds(pl.multiple_of(place[2] * cols, cols), cols)]
    for k, parcel in enumerate(parcels):
        parcel[...] = tokens[:, pl.ds(pl.multiple_of(place[3 + k] * cols, cols), cols)]


def choose(values, eps):
    ids = lax.broadcasted_iota(jnp.int32, values.shape, 1).astype(jnp.float32)
    top = jnp.max(values, axis=1, keepdims=True)
    choice = jnp.min(jnp.where(values == top, ids, far), axis=1, keepdims=True)
    claims = ids == choice
    second = jnp.max(jnp.where(claims, lowest, values), axis=1, keepdims=True)
    bids = jnp.where(claims, top - second + eps, -1.0)
    return choice, claims, bids, jnp.max(bids, axis=0, keepdims=True)


def first_round(place, kept, theirs, epsilon, values, out):
    if theirs is None:
        values[...] = kept[...]
    else:
        own = kept.shape[1]
        swapped = place[0] != 0
        values[:, :own] = jnp.where(swapped, theirs[...], kept[...])
        values[:, own:] = jnp.where(swapped, kept[...], theirs[...])
    raised = choose(values[...], epsilon[0])[-1]
    out[...] = jnp.broadcast_to(raised[None], out.shape)


def first_round_whole(place, kept, epsilon, values, out):
    first_round(place, kept, None, epsilon, values, out)


def next_round(values, before, epsilon, bids, out, after):
    total = before[...] + jnp.maximum(jnp.max(bids[...], axis=0), 0.0)
    after[...] = total
    raised = choose(values[...] - total, epsilon[0])[-1]
    out[...] = jnp.broadcast_to(raised[None], out.shape)


def last_round(values, before, epsilon, bids, base, out, after):
    rows, experts = values.shape
    total = before[...] + jnp.maximum(jnp.max(bids[...], axis=0), 0.0)
    after[...] = total
    choice, claims, spread, raised = choose(values[...] - total, epsilon[0])
    token = (base[0] + lax.broadcasted_iota(jnp.int32, (rows, experts), 0)).astype(jnp.float32)
    first = jnp.min(jnp.where(claims & (spread == raised), token, far), axis=0, keepdims=True)
    count = jnp.sum(claims.astype(jnp.float32), axis=0, keepdims=True)
    wide = out.shape[2] - 3 * experts
    lane = lax.broadcasted_iota(jnp.int32, (rows, wide), 1)
    row = lax.broadcasted_iota(jnp.int32, (rows, wide), 0)
    turned = jnp.sum(jnp.where(lane == row, choice, 0.0), axis=0, keepdims=True)
    line = jnp.concatenate([raised, first, count, turned], axis=1)
    out[...] = jnp.broadcast_to(line[None], out.shape)


def finish(ne, rows, place, info, before, prices, centroids, *refs):
    columns, (final, holder, best, block) = refs[:-4], refs[-4:]
    experts = before.shape[1]
    own = centroids.shape[0]
    start = place[0]
    if own % 128 == 0:
        start = pl.multiple_of(start, 128)
        raised = info[:, :, pl.ds(start, own)]
        firsts = info[:, :, pl.ds(pl.multiple_of(experts + start, 128), own)]
        earlier = before[:, pl.ds(start, own)]
        top_bid = jnp.max(raised, axis=0)
        first = jnp.min(jnp.where(raised == top_bid[None], firsts, far), axis=0)
        final[...] = prices[...] + earlier + jnp.maximum(top_bid, 0.0)
        holder[...] = jnp.where(top_bid > 0, first, -1.0).astype(jnp.int32)
    else:
        raised = info[:, :, :experts]
        top_bid = jnp.max(raised, axis=0)
        firsts = jnp.where(raised == top_bid[None], info[:, :, experts : 2 * experts], far)
        final[...] = before[...] + jnp.maximum(top_bid, 0.0)
        holder[...] = jnp.where(top_bid > 0, jnp.min(firsts, axis=0), -1.0).astype(jnp.int32)
    for c in range(ne):
        best[c] = info[place[1] * ne + c, :, 3 * experts : 3 * experts + rows].astype(jnp.int32)
    ids = (start + lax.broadcasted_iota(jnp.int32, (own, rows), 0)).astype(jnp.float32)
    total = jnp.zeros(block.shape, jnp.float32)
    for k, features in enumerate(columns):
        for c in range(ne):
            chosen = info[place[2 + k] * ne + c, :, 3 * experts : 3 * experts + rows]
            hot = jnp.where(ids == chosen, 1.0, 0.0).astype(jnp.bfloat16)
            total += jnp.dot(
                hot, features[c * rows : (c + 1) * rows, :], preferred_element_type=jnp.float32
            )
    counts = jnp.sum(info[:, :, 2 * experts : 3 * experts], axis=0)
    expert_row = place[0] + lax.broadcasted_iota(jnp.int32, (own, experts), 0)
    lane = lax.broadcasted_iota(jnp.int32, (own, experts), 1)
    counts = jnp.sum(jnp.where(expert_row == lane, counts, 0.0), axis=1, keepdims=True)
    fresh = 0.5 * centroids[...].astype(jnp.float32) + 0.5 * total / jnp.maximum(counts, 1.0)
    block[...] = fresh.astype(block.dtype)


def assemble(plan, base, *refs):
    pieces, out, sem = refs[:-2], refs[-2], refs[-1]
    cols = pieces[0].shape[-1]
    copies = []
    for piece, slots in zip(pieces, plan):
        for i, slot in enumerate(slots):
            col = pl.multiple_of(base[slot] * cols, cols)
            source = piece if len(piece.shape) == 2 else piece.at[i]
            copies.append(
                pltpu.make_async_copy(source, out.at[:, pl.ds(col, cols)], sem.at[len(copies)])
            )
    for copy in copies:
        copy.start()
    for copy in copies:
        copy.wait()


def gather_columns(block, n, ne):
    if ne != 2 or n % 4 or block.shape[1] % 128:
        return lax.all_gather(block, "dp", axis=1, tiled=True)
    line = n // 4
    me, core = lax.axis_index("dp"), lax.axis_index("expert")

    def move(value, steps, flips):
        pairs = []
        for i in range(n):
            for c in range(2):
                to = (i // 4 + steps[c]) % line * 4 + (i % 4 ^ flips[c])
                pairs.append((i * 2 + c, to * 2 + c))
        return lax.ppermute(value, ("dp", "expert"), pairs)

    across, along = (1, 2), (2, 1)
    got, held = [(block, [(0, 0)])], [("a", None)]

    def stack(values):
        values = [v if v.ndim == 3 else v[None] for v in values]
        return values[0] if len(values) == 1 else jnp.concatenate(values)

    def flip(offsets, kinds):
        return [(o, k) for o, k in zip(offsets, kinds)]

    def first_flip(values, offsets):
        value = move(stack(values), (0, 0), across)
        got.append((value, [(o, 1) for o in offsets]))
        return value

    def second_flip(values, slots):
        value = move(stack(values), (0, 0), along)
        got.append((value, [(o, code + 2) for o, code in slots]))

    up, down = move(block, (1, 1), (0, 0)), move(block, (-1, -1), (0, 0))
    plane = first_flip([block], [0])
    second_flip([block, plane], [(0, 0), (0, 1)])
    if line >= 3:
        for s in range(1, (line - 1) // 2 + 1):
            if s > 1:
                up, down = move(up, (1, 1), (0, 0)), move(down, (-1, -1), (0, 0))
            got += [(up, [(-s, 0)]), (down, [(s, 0)])]
            plane = first_flip([up, down], [-s, s])
            second_flip([up, down, plane], [(-s, 0), (s, 0), (-s, 1), (s, 1)])
    if line % 2 == 0:
        s = line // 2
        lasting = move(jnp.where(core == 0, up, down), (1, -1), (0, 0)) if line > 2 else up
        got.append((lasting, [(s, 0)]))
        plane = first_flip([lasting], [s])
        second_flip([lasting, plane], [(s, 0), (s, 1)])

    slots = sorted({slot for _, entry in got for slot in entry})
    one, two = 1 + core, 2 - core
    codes = [0, one, two, 3]
    base = jnp.stack([(me // 4 + o) % line * 4 + (me % 4 ^ codes[f]) for o, f in slots]).astype(jnp.int32)
    plan = [[slots.index(slot) for slot in entry] for _, entry in got]
    own, cols = block.shape
    return pl.pallas_call(
        functools.partial(assemble, plan),
        out_shape=jax.ShapeDtypeStruct((own, n * cols), block.dtype),
        in_specs=[SMEM] + [VMEM] * len(got),
        out_specs=ANY,
        scratch_shapes=[pltpu.SemaphoreType.DMA((sum(map(len, plan)),))],
        compiler_params=ROOM,
        name="assemble",
    )(base, *[value for value, _ in got])


def body(dp, ne, tokens, centroids, prices, epsilon):
    f32 = jnp.float32
    local_tokens, width = tokens.shape
    own = centroids.shape[0]
    experts = own * ne
    devices = dp * ne
    rows = local_tokens // ne
    cols = width // dp
    dp_at, expert_at = lax.axis_index("dp"), lax.axis_index("expert")
    everywhere = ("dp", "expert")
    paired = ne == 2 and dp & (dp - 1) == 0 and dp > 1 and cols % 128 == 0
    swap = [(0, 1), (1, 0)]

    def shape(*sizes, dtype=f32):
        return jax.ShapeDtypeStruct(sizes, dtype)

    line, spread = shape(1, experts), shape(devices, 1, experts)
    at = jnp.stack([expert_at]).astype(jnp.int32)
    if paired:
        half = dp // 2
        theirs = [dp_at ^ (2 * k + expert_at) for k in range(half)]
        place = jnp.stack([expert_at, 1 - expert_at, dp_at] + theirs).astype(jnp.int32)
        kept, sent, mine, *parcels = pl.pallas_call(
            opening,
            out_shape=[shape(rows, own)] * 2
            + [shape(own, cols, dtype=centroids.dtype)]
            + [shape(local_tokens, cols, dtype=tokens.dtype)] * half,
            in_specs=[SMEM, VMEM, VMEM, VMEM],
            out_specs=[VMEM] * (3 + half),
            compiler_params=ROOM,
            name="opening",
        )(place, tokens, centroids, prices.reshape(1, own))
        received = lax.ppermute(sent, "expert", swap)
        values, bids = pl.pallas_call(
            first_round,
            out_shape=(shape(rows, experts), spread),
            in_specs=[SMEM, VMEM, VMEM, SMEM],
            out_specs=(VMEM, VMEM),
            name="first_round",
        )(at, kept, received, epsilon)
        columns = []
        for k, parcel in enumerate(parcels):
            pairs = [
                (i * 2 + c, (i ^ (2 * k + c)) * 2 + c) for i in range(dp) for c in range(2)
            ]
            columns.append(lax.ppermute(parcel, everywhere, pairs))
        columns += [lax.ppermute(c, "expert", swap) for c in columns]
        sources = theirs + [dp_at ^ (2 * k + 1 - expert_at) for k in range(half)]
    else:
        parcels = tokens.reshape(local_tokens, dp, cols).transpose(1, 0, 2)
        columns = lax.all_to_all(parcels, "dp", 0, 0, tiled=True)
        columns = [columns.reshape(dp * local_tokens, cols)[i * local_tokens :][:local_tokens] for i in range(dp)]
        sources = list(range(dp))
        mine = lax.dynamic_slice_in_dim(centroids, dp_at * cols, cols, 1)
        part = lax.dot_general(
            tokens, centroids, (((1,), (1,)), ((), ())), preferred_element_type=f32
        ) * 0.015625 - prices
        part = lax.all_to_all(part, "expert", 0, 1, tiled=True)
        values, bids = pl.pallas_call(
            first_round_whole,
            out_shape=(shape(rows, experts), spread),
            in_specs=[SMEM, VMEM, SMEM],
            out_specs=(VMEM, VMEM),
            name="first_round",
        )(at, part, epsilon)

    total = jnp.zeros((1, experts), f32)
    for _ in range(ROUNDS - 2):
        bids = lax.all_to_all(bids, everywhere, 0, 0, tiled=True)
        bids, total = pl.pallas_call(
            next_round,
            out_shape=(spread, line),
            in_specs=[VMEM, VMEM, SMEM, VMEM],
            out_specs=(VMEM, VMEM),
            name="next_round",
        )(values, total, epsilon, bids)
    bids = lax.all_to_all(bids, everywhere, 0, 0, tiled=True)
    wide = -(-rows // 128) * 128
    base = (dp_at * local_tokens + expert_at * rows).astype(jnp.int32).reshape(1)
    info, total = pl.pallas_call(
        last_round,
        out_shape=(shape(devices, 1, 3 * experts + wide), line),
        in_specs=[VMEM, VMEM, SMEM, VMEM, SMEM],
        out_specs=(VMEM, VMEM),
        name="last_round",
    )(values, total, epsilon, bids, base)
    info = lax.all_to_all(info, everywhere, 0, 0, tiled=True)

    place = jnp.stack([expert_at * own, dp_at] + sources).astype(jnp.int32)
    direct = own % 128 == 0
    listed = own if direct else experts
    final, holder, best, block = pl.pallas_call(
        functools.partial(finish, ne, rows),
        out_shape=(
            shape(1, listed),
            shape(1, listed, dtype=jnp.int32),
            shape(ne, 1, rows, dtype=jnp.int32),
            shape(own, cols, dtype=centroids.dtype),
        ),
        in_specs=[SMEM] + [VMEM] * (4 + len(columns)),
        out_specs=(VMEM, VMEM, VMEM, VMEM),
        compiler_params=ROOM,
        name="finish",
    )(place, info, total, prices.reshape(1, own), mine, *columns)
    refreshed = gather_columns(block, dp, ne)
    if direct:
        final, holder = final[0], holder[0]
    else:
        final = prices + lax.dynamic_slice_in_dim(final[0], expert_at * own, own, 0)
        holder = lax.dynamic_slice_in_dim(holder[0], expert_at * own, own, 0)
    return final, best.reshape(local_tokens), holder, refreshed


def solution(mesh):
    placed = (P("dp", None), P("expert", None), P("expert"), P())
    return jax.shard_map(
        functools.partial(body, mesh.shape["dp"], mesh.shape["expert"]),
        mesh=mesh,
        in_specs=placed,
        out_specs=(P("expert"), P("dp"), P("expert"), P("expert", None)),
        check_vma=False,
    )
```

time: 204 us -> 122 us (0.60)
  Pallas kernels: 74.7 us -> 12.5 us
  blocking collectives: 57.8 us -> 0 us
  starting transfers between devices: 24.8 us -> 47.5 us
  waiting for transfers between devices: 27.9 us -> 49.9 us
  other arithmetic: 3.26 us -> 0.17 us
  local copies, waits for them, and re-layouts: 12.5 us -> 9.92 us
    pallas_call x1, Pallas kernels: 65.6 us -> 1.98 us  [gather_columns(): pl.pallas_call(functools.partial(assemble, plan), out_shape=jax.ShapeDtyp...]
    all_to_all x2 -> x0, blocking collectives: 55.9 us -> none  [the longest x1 45.2 us: body(): columns = lax.all_to_all(parcels, everywhere, 0, 0, tiled=True)]
    ppermute x18 -> x26, waiting for transfers between devices: 12.3 us -> 36.9 us  [the longest x9 23.8 us: move(): return lax.ppermute(value, ('dp', 'expert'), pairs)]
    all_to_all x1 -> x2, starting transfers between devices: 2.55 us -> 13.3 us  [body(): bids = lax.all_to_all(bids, everywhere, 0, 0, tiled=True)]
    ppermute x18 -> x26, starting transfers between devices: 19.6 us -> 30.2 us  [the longest x9 14.3 us: move(): return lax.ppermute(value, ('dp', 'expert'), pairs)]
    all_to_all x1, waiting for transfers between devices: 8.17 us -> 0.01 us  [body(): info = lax.all_to_all(info, everywhere, 0, 0, tiled=True)]
    all_to_all x1 -> x2, waiting for transfers between devices: 7.4 us -> 13 us  [body(): bids = lax.all_to_all(bids, everywhere, 0, 0, tiled=True)]
    dynamic_slice x4 -> x0, local copies, waits for them, and re-layouts: 3.39 us -> none  [the longest x1 1.57 us: body(): my_centroids = lax.dynamic_slice_in_dim(centroids, dp_at * cols, cols, 1)]
  transfers between devices with their start and end apart: 20 -> 29, of which waited for: 8 -> 14; matrix products, arithmetic and copies ran while one was open for 5% -> 1% of each run, Pallas kernels for 3% -> 5%
where the time goes in v2:
time: 122 us; the launch traced here: 121 us
  waiting for transfers between devices  49.9 us (41%)
  starting transfers between devices  47.5 us (39%)
  Pallas kernels  12.5 us (10%)
  local copies, waits for them, and re-layouts  9.92 us (8%)
  between operations  1.46 us (1%)
    ppermute x9, waiting for transfers between devices, move(): return lax.ppermute(value, ('dp', 'expert'), pairs)  23.8 us
    ppermute x9, starting transfers between devices, move(): return lax.ppermute(value, ('dp', 'expert'), pairs)  14.3 us
    ppermute x8, starting transfers between devices, body(): columns.append(lax.ppermute(parcel, everywhere, pairs))  13.4 us
    all_to_all x2, starting transfers between devices, body(): bids = lax.all_to_all(bids, everywhere, 0, 0, tiled=True)  13.3 us
    all_to_all x2, waiting for transfers between devices, body(): bids = lax.all_to_all(bids, everywhere, 0, 0, tiled=True)  13 us
    ppermute x8, waiting for transfers between devices, body(): columns.append(lax.ppermute(parcel, everywhere, pairs))  11.9 us
    unnamed x22, local copies, waits for them, and re-layouts  8.39 us
    all_to_all x1, starting transfers between devices, body(): info = lax.all_to_all(info, everywhere, 0, 0, tiled=True)  4.01 us
  transfers between devices with their start and end apart: 29, of which 14 were waited for; matrix products, arithmetic and copies ran while one was open for 1% of the time, Pallas kernels for 5%

profile of v2, /device:TPU:0, one launch (start us, length us, event | category | flops | bytes accessed | tf_op | source)
XLA Modules:
  0.0 121.4 jit_solution(8616812034690256104)
XLA Ops:
  0.7 1.9 %copy-done = bf16[384,4096]{1,0:T(8,128)(2,1)S(1)} copy-done((bf16[384,4096]{1,0:T(8,128)(2,1)S(1)}, bf16[384,4096]{1,0:T(8,128)(2,1)}, u32[]{:S(2)}) %copy-start) | copy-done | bytes 3145752
  2.6 1.6 %copy-done.1 = bf16[256,4096]{1,0:T(8,128)(2,1)S(1)} copy-done((bf16[256,4096]{1,0:T(8,128)(2,1)S(1)}, bf16[256,4096]{1,0:T(8,128)(2,1)}, u32[]{:S(2)}) %copy-start.1) | copy-done | bytes 2097176
  4.2 0.7 copy-done.5
  4.9 2.2 %opening.1 = (f32[192,256]{1,0:T(8,128)S(1)}, f32[192,256]{1,0:T(8,128)S(1)}, bf16[256,256]{1,0:T(8,128)(2,1)S(1)}, bf16[384,256]{1,0:T(8,128)(2,1)S(1)}, bf16[3...) custom-call(s32[11]{0:T(128)S(1)} %stack.148.place, ...), custom_call_target="tpu_custom_call" | custom-call | tf_op jit(solution)/shard_map/opening/pallas_call | solution.py:231
  7.1 0.7 copy-done.2
  7.8 0.6 copy-done.3
  8.4 0.5 collective-permute-start
  8.9 0.7 collective-permute-start.1
  10.2 0.7 copy-done.10
  10.9 2.0 %first_round.1 = (f32[192,512]{1,0:T(8,128)}, f32[32,1,512]{2,1,0:T(1,128)}) custom-call(s32[1]{0:T(128)} %bitcast.18.place, f32[192,256]{1,0:T(8,128)} %copy-done.2, f32[192,256]{1,0:T(8,128)} %copy-done.10, f32[1]{0:T(128)S(6)} %copy.8.epsilon), custom_call_target="tpu_custom_call" | custom-call | tf_op jit(solution)/shard_map/first_round/pallas_call | solution.py:242
  12.8 8.5 %all-to-all-start = ((f32[32,1,512]{2,1,0:T(1,128)}), f32[32,1,512]{2,1,0:T(1,128)S(1)}, u32[]{:S(2)}, u32[]{:S(2)}) async-start(f32[32,1,512]{2,1,0:T(1,128)} %get-tuple-element.28), calls=%async_computation | async-start | bytes 131072 | tf_op jit(solution)/shard_map/all_to_all | solution.py:277
  21.3 1.8 %collective-permute-start.2 = (bf16[384,256]{1,0:T(8,128)(2,1)S(1)}, bf16[384,256]{1,0:T(8,128)(2,1)S(1)}, u32[]{:S(2)}, u32[]{:S(2)}) collective-permute-start(bf16[384,256]{1,0:T(8,128)(2,1)S(1)} %get-tuple-element.35), channel_id=1, source_target_pairs={{0,4},{1,7},{2,6},{3,5},{4,0},{5,3},{6,2},{7,1},{8,12},{9,15},{10,... | collective-permute-start | bytes 589832 | tf_op jit(solution)/shard_map/ppermute | solution.py:254
  23.1 1.5 %collective-permute-start.3 = (bf16[384,256]{1,0:T(8,128)(2,1)S(1)}, bf16[384,256]{1,0:T(8,128)(2,1)S(1)}, u32[]{:S(2)}, u32[]{:S(2)}) collective-permute-start(bf16[384,256]{1,0:T(8,128)(2,1)S(1)} %get-tuple-element.36), channel_id=1, source_target_pairs={{0,8},{1,11},{2,10},{3,9},{4,12},{5,15},{6,14},{7,13},{8,0},{9,3},... | collective-permute-start | bytes 589832 | tf_op jit(solution)/shard_map/ppermute | solution.py:254
  24.9 2.7 %collective-permute-start.5 = (bf16[384,256]{1,0:T(8,128)(2,1)S(1)}, bf16[384,256]{1,0:T(8,128)(2,1)S(1)}, u32[]{:S(2)}, u32[]{:S(2)}) collective-permute-start(bf16[384,256]{1,0:T(8,128)(2,1)S(1)} %get-tuple-element.38), channel_id=1, source_target_pairs={{0,16},{1,19},{2,18},{3,17},{4,20},{5,23},{6,22},{7,21},{8,24},{9,... | collective-permute-start | bytes 589832 | tf_op jit(solution)/shard_map/ppermute | solution.py:254
  27.5 1.5 %collective-permute-start.6 = (bf16[384,256]{1,0:T(8,128)(2,1)S(1)}, bf16[384,256]{1,0:T(8,128)(2,1)S(1)}, u32[]{:S(2)}, u32[]{:S(2)}) collective-permute-start(bf16[384,256]{1,0:T(8,128)(2,1)S(1)} %get-tuple-element.39), channel_id=1, source_target_pairs={{0,20},{1,23},{2,22},{3,21},{4,16},{5,19},{6,18},{7,17},{8,28},{9,... | collective-permute-start | bytes 589832 | tf_op jit(solution)/shard_map/ppermute | solution.py:254
  29.0 0.6 broadcast_in_dim.19.before
  29.6 1.9 %next_round.1 = (f32[32,1,512]{2,1,0:T(1,128)}, f32[1,512]{1,0:T(1,128)}) custom-call(f32[192,512]{1,0:T(8,128)} %get-tuple-element.27.values, f32[1,512]{1,0:T(1,128)} %broadcast_in_dim.19.before, f32[1]{0:T(128)S(6)} %copy.8.epsilon, f32[32,1,512]{2,1,0:T(1,128)} %copy-done.9), custom_call_target="tpu_custom_call" | custom-call | tf_op jit(solution)/shard_map/next_round/pallas_call | solution.py:278
  31.6 4.8 %all-to-all-start.1 = ((f32[32,1,512]{2,1,0:T(1,128)}), f32[32,1,512]{2,1,0:T(1,128)S(1)}, u32[]{:S(2)}, u32[]{:S(2)}) async-start(f32[32,1,512]{2,1,0:T(1,128)} %get-tuple-element.30), calls=%async_computation.1 | async-start | bytes 131072 | tf_op jit(solution)/shard_map/all_to_all | solution.py:285
  36.4 13.0 %all-to-all-done.1.bids = f32[32,1,512]{2,1,0:T(1,128)S(1)} async-done(((f32[32,1,512]{2,1,0:T(1,128)}), f32[32,1,512]{2,1,0:T(1,128)S(1)}, u32[]{:S(2)}, u32[]{:S(2)}) %all-to-all-start.1) | async-done | bytes 65568 | tf_op jit(solution)/shard_map/all_to_all | solution.py:285
  49.4 0.6 copy-done.8
  50.0 2.1 %last_round.1 = (f32[32,1,1792]{2,1,0:T(1,128)}, f32[1,512]{1,0:T(1,128)}) custom-call(f32[192,512]{1,0:T(8,128)} %get-tuple-element.27.values, f32[1,512]{1,0:T(1,128)} %get-tuple-element.29.before, f32[1]{0:T(128)S(6)} %copy.8.epsilon, f32[32,1,512]{2,1,0:T(1,128)} %copy-done.8, s32[1]{0:T(128)} %bitcast.21.base), custom_call_target="tpu_custom_call" | custom-call | tf_op jit(solution)/shard_map/last_round/pallas_call | solution.py:288
  52.1 4.0 %all-to-all-start.2 = ((f32[32,1,1792]{2,1,0:T(1,128)}), f32[32,1,1792]{2,1,0:T(1,128)S(1)}, u32[]{:S(2)}, u32[]{:S(2)}) async-start(f32[32,1,1792]{2,1,0:T(1,128)} %get-tuple-element.31), calls=%async_computation.2 | async-start | bytes 458752 | tf_op jit(solution)/shard_map/all_to_all | solution.py:295
  56.2 3.7 %collective-permute-start.7 = (bf16[384,256]{1,0:T(8,128)(2,1)S(1)}, bf16[384,256]{1,0:T(8,128)(2,1)S(1)}, u32[]{:S(2)}, u32[]{:S(2)}) collective-permute-start(bf16[384,256]{1,0:T(8,128)(2,1)S(1)} %get-tuple-element.40), channel_id=1, source_target_pairs={{0,24},{1,27},{2,26},{3,25},{4,28},{5,31},{6,30},{7,29},{8,16},{9,... | collective-permute-start | bytes 589832 | tf_op jit(solution)/shard_map/ppermute | solution.py:254
  59.8 1.4 %collective-permute-start.8 = (bf16[384,256]{1,0:T(8,128)(2,1)S(1)}, bf16[384,256]{1,0:T(8,128)(2,1)S(1)}, u32[]{:S(2)}, u32[]{:S(2)}) collective-permute-start(bf16[384,256]{1,0:T(8,128)(2,1)S(1)} %get-tuple-element.41), channel_id=1, source_target_pairs={{0,28},{1,31},{2,30},{3,29},{4,24},{5,27},{6,26},{7,25},{8,20},{9,... | collective-permute-start | bytes 589832 | tf_op jit(solution)/shard_map/ppermute | solution.py:254
  61.3 0.5 collective-permute-start.9
  61.8 0.4 collective-permute-start.11
  62.3 7.0 %collective-permute-done.7.refs_6_ = bf16[384,256]{1,0:T(8,128)(2,1)S(1)} collective-permute-done((bf16[384,256]{1,0:T(8,128)(2,1)S(1)}, bf16[384,256]{1,0:T(8,128)(2,1)S(1)}, u32[]{:S(2)}, u32[]{:S(2)}) %collective-permute-start.7) | collective-permute-done | bytes 196640 | tf_op jit(solution)/shard_map/ppermute | solution.py:254
  69.2 4.9 %collective-permute-done.8.refs_7_ = bf16[384,256]{1,0:T(8,128)(2,1)S(1)} collective-permute-done((bf16[384,256]{1,0:T(8,128)(2,1)S(1)}, bf16[384,256]{1,0:T(8,128)(2,1)S(1)}, u32[]{:S(2)}, u32[]{:S(2)}) %collective-permute-start.8) | collective-permute-done | bytes 196640 | tf_op jit(solution)/shard_map/ppermute | solution.py:254
  74.3 0.4 collective-permute-start.14
  76.4 0.9 copy-done.4
  77.4 0.7 copy-done.7
  78.0 2.3 %finish.1 = (f32[1,256]{1,0:T(1,128)}, s32[1,256]{1,0:T(1,128)}, s32[2,1,192]{2,1,0:T(1,128)S(1)}, bf16[256,256]{1,0:T(8,128)(2,1)S(1)}) custom-call(s32[18]{0:T(128)S(1)} %stack.145.place, f32[32,1,1792]{2,1,0:T(1,128)S(1)} %all-to-all-done.2.info, f32[1,512]{1,0:T(1,128)S(1)} %copy-done.7, f32[1,256]{1,0:T(1,128)S(1)} %bitcast.53, ...), custom_call_target="tpu_custom_call" | custom-call | tf_op jit(solution)/shard_map/finish/pallas_call | solution.py:300
  80.7 8.9 %collective-permute-start.19 = (bf16[256,256]{1,0:T(8,128)(2,1)S(1)}, bf16[256,256]{1,0:T(8,128)(2,1)S(1)}, u32[]{:S(2)}, u32[]{:S(2)}) collective-permute-start(bf16[256,256]{1,0:T(8,128)(2,1)S(1)} %get-tuple-element.45.refs_0_), channel_id=1, source_target_pairs={{0,8},{1,9},{2,10},{3,11},{4,12},{5,13},{6,14},{7,15},{8,16},{9,17... | collective-permute-start | bytes 393224 | tf_op jit(solution)/shard_map/ppermute | solution.py:154
  89.6 3.9 %collective-permute-done.20.refs_4_ = bf16[256,256]{1,0:T(8,128)(2,1)S(1)} collective-permute-done((bf16[256,256]{1,0:T(8,128)(2,1)S(1)}, bf16[256,256]{1,0:T(8,128)(2,1)S(1)}, u32[]{:S(2)}, u32[]{:S(2)}) %collective-permute-start.20) | collective-permute-done | bytes 131104 | tf_op jit(solution)/shard_map/ppermute | solution.py:154
  93.5 4.1 %collective-permute-done.19.refs_3_ = bf16[256,256]{1,0:T(8,128)(2,1)S(1)} collective-permute-done((bf16[256,256]{1,0:T(8,128)(2,1)S(1)}, bf16[256,256]{1,0:T(8,128)(2,1)S(1)}, u32[]{:S(2)}, u32[]{:S(2)}) %collective-permute-start.19) | collective-permute-done | bytes 131104 | tf_op jit(solution)/shard_map/ppermute | solution.py:154
  97.6 1.2 %collective-permute-start.21 = (bf16[2,256,256]{2,1,0:T(8,128)(2,1)S(1)}, bf16[2,256,256]{2,1,0:T(8,128)(2,1)S(1)}, u32[]{:S(2)}, u32[]{:S(2)}) collective-permute-start(bf16[2,256,256]{2,1,0:T(8,128)(2,1)S(1)} %pad_maximum_fusion.2), channel_id=1, source_target_pairs={{0,2},{1,5},{2,0},{3,7},{4,6},{5,1},{6,4},{7,3},{8,10},{9,13},{10,... | collective-permute-start | bytes 786440 | tf_op jit(solution)/shard_map/ppermute | solution.py:154
  98.8 0.9 collective-permute-start.17
  99.8 4.3 %collective-permute-done.21.refs_5_ = bf16[2,256,256]{2,1,0:T(8,128)(2,1)S(1)} collective-permute-done((bf16[2,256,256]{2,1,0:T(8,128)(2,1)S(1)}, bf16[2,256,256]{2,1,0:T(8,128)(2,1)S(1)}, u32[]{:S(2)}, u32[]{:S(2)}) %collective-permute-start.21) | collective-permute-done | bytes 262176 | tf_op jit(solution)/shard_map/ppermute | solution.py:154
  104.1 0.6 collective-permute-start.22
  104.7 1.9 %collective-permute-done.23.refs_7_ = bf16[256,256]{1,0:T(8,128)(2,1)S(1)} collective-permute-done((bf16[256,256]{1,0:T(8,128)(2,1)S(1)}, bf16[256,256]{1,0:T(8,128)(2,1)S(1)}, u32[]{:S(2)}, u32[]{:S(2)}) %collective-permute-start.23) | collective-permute-done | bytes 131104 | tf_op jit(solution)/shard_map/ppermute | solution.py:154
  106.5 1.2 collective-permute-start.24
  107.7 0.6 collective-permute-start.18
  108.3 4.6 %collective-permute-done.24.refs_8_ = bf16[1,256,256]{2,1,0:T(8,128)(2,1)S(1)} collective-permute-done((bf16[1,256,256]{2,1,0:T(8,128)(2,1)S(1)}, bf16[1,256,256]{2,1,0:T(8,128)(2,1)S(1)}, u32[]{:S(2)}, u32[]{:S(2)}) %collective-permute-start.24) | collective-permute-done | bytes 131104 | tf_op jit(solution)/shard_map/ppermute | solution.py:154
  113.0 0.6 collective-permute-start.25
  113.7 0.7 reshape.20
  114.3 1.8 %collective-permute-done.18.refs_2_ = bf16[2,256,256]{2,1,0:T(8,128)(2,1)S(1)} collective-permute-done((bf16[2,256,256]{2,1,0:T(8,128)(2,1)S(1)}, bf16[2,256,256]{2,1,0:T(8,128)(2,1)S(1)}, u32[]{:S(2)}, u32[]{:S(2)}) %collective-permute-start.18) | collective-permute-done | bytes 262176 | tf_op jit(solution)/shard_map/ppermute | solution.py:154
  116.2 3.3 %collective-permute-done.25.refs_9_ = bf16[2,256,256]{2,1,0:T(8,128)(2,1)S(1)} collective-permute-done((bf16[2,256,256]{2,1,0:T(8,128)(2,1)S(1)}, bf16[2,256,256]{2,1,0:T(8,128)(2,1)S(1)}, u32[]{:S(2)}, u32[]{:S(2)}) %collective-permute-start.25) | collective-permute-done | bytes 262176 | tf_op jit(solution)/shard_map/ppermute | solution.py:154
  119.4 2.0 %assemble.1 = bf16[256,4096]{1,0:T(8,128)(2,1)} custom-call(s32[16]{0:T(128)S(1)} %stack.165.base, bf16[256,256]{1,0:T(8,128)(2,1)S(1)} %get-tuple-element.45.refs_0_, bf16[1,256,256]{2,1,0:T(8,128)(2,1)S(1)} %collective-permute-done.17.refs_1_, bf16[2,256,256]{2,1,0:T(8,128)(2,1)S(1)} %collective-permute-done.18.refs_2_, ...), custom_call_target="tpu_custom_call" | custom-call | tf_op jit(solution)/shard_map/assemble/pallas_call | solution.py:198
  (49 shorter events, 3.0 us)
Async XLA Ops:
  0.7 1.9 %copy-start = (bf16[384,4096]{1,0:T(8,128)(2,1)S(1)}, bf16[384,4096]{1,0:T(8,128)(2,1)}, u32[]{:S(2)}) copy-start(bf16[384,4096]{1,0:T(8,128)(2,1)} %tokens.1) | copy-start | bytes 9437188
  2.6 1.6 %copy-start.1 = (bf16[256,4096]{1,0:T(8,128)(2,1)S(1)}, bf16[256,4096]{1,0:T(8,128)(2,1)}, u32[]{:S(2)}) copy-start(bf16[256,4096]{1,0:T(8,128)(2,1)} %centroids.1) | copy-start | bytes 6291460
  4.2 0.7 copy-start.5
  7.1 0.7 copy-start.2
  7.8 0.6 copy-start.3
  8.4 68.0 %copy-start.6 = (f32[256]{0:T(256)S(1)}, f32[256]{0:T(256)}, u32[]{:S(2)}) copy-start(f32[256]{0:T(256)} %param.6) | copy-start | bytes 3076
  8.4 1.8 %collective-permute-start = (f32[192,256]{1,0:T(8,128)S(1)}, f32[192,256]{1,0:T(8,128)S(1)}, u32[]{:S(2)}, u32[]{:S(2)}) collective-permute-start(f32[192,256]{1,0:T(8,128)S(1)} %get-tuple-element.26), channel_id=1, source_target_pairs={{0,1},{1,0},{2,3},{3,2},{4,5},{5,4},{6,7},{7,6},{8,9},{9,8},{10,11... | collective-permute-start | bytes 589832 | tf_op jit(solution)/shard_map/ppermute | solution.py:241
  8.9 18.7 %collective-permute-start.1 = (bf16[384,256]{1,0:T(8,128)(2,1)S(1)}, bf16[384,256]{1,0:T(8,128)(2,1)S(1)}, u32[]{:S(2)}, u32[]{:S(2)}) collective-permute-start(bf16[384,256]{1,0:T(8,128)(2,1)S(1)} %get-tuple-element.34), channel_id=1, source_target_pairs={{0,0},{1,3},{2,2},{3,1},{4,4},{5,7},{6,6},{7,5},{8,8},{9,11},{10,1... | collective-permute-start | bytes 589832 | tf_op jit(solution)/shard_map/ppermute | solution.py:254
  10.2 0.7 copy-start.10
  12.8 16.2 %all-to-all-start = ((f32[32,1,512]{2,1,0:T(1,128)}), f32[32,1,512]{2,1,0:T(1,128)S(1)}, u32[]{:S(2)}, u32[]{:S(2)}) async-start(f32[32,1,512]{2,1,0:T(1,128)} %get-tuple-element.28), calls=%async_computation | async-start | bytes 131072 | tf_op jit(solution)/shard_map/all_to_all | solution.py:277
  21.3 34.8 %collective-permute-start.2 = (bf16[384,256]{1,0:T(8,128)(2,1)S(1)}, bf16[384,256]{1,0:T(8,128)(2,1)S(1)}, u32[]{:S(2)}, u32[]{:S(2)}) collective-permute-start(bf16[384,256]{1,0:T(8,128)(2,1)S(1)} %get-tuple-element.35), channel_id=1, source_target_pairs={{0,4},{1,7},{2,6},{3,5},{4,0},{5,3},{6,2},{7,1},{8,12},{9,15},{10,... | collective-permute-start | bytes 589832 | tf_op jit(solution)/shard_map/ppermute | solution.py:254
  23.1 36.7 %collective-permute-start.3 = (bf16[384,256]{1,0:T(8,128)(2,1)S(1)}, bf16[384,256]{1,0:T(8,128)(2,1)S(1)}, u32[]{:S(2)}, u32[]{:S(2)}) collective-permute-start(bf16[384,256]{1,0:T(8,128)(2,1)S(1)} %get-tuple-element.36), channel_id=1, source_target_pairs={{0,8},{1,11},{2,10},{3,9},{4,12},{5,15},{6,14},{7,13},{8,0},{9,3},... | collective-permute-start | bytes 589832 | tf_op jit(solution)/shard_map/ppermute | solution.py:254
  24.6 36.7 %collective-permute-start.4 = (bf16[384,256]{1,0:T(8,128)(2,1)S(1)}, bf16[384,256]{1,0:T(8,128)(2,1)S(1)}, u32[]{:S(2)}, u32[]{:S(2)}) collective-permute-start(bf16[384,256]{1,0:T(8,128)(2,1)S(1)} %get-tuple-element.37), channel_id=1, source_target_pairs={{0,12},{1,15},{2,14},{3,13},{4,8},{5,11},{6,10},{7,9},{8,4},{9,7},... | collective-permute-start | bytes 589832 | tf_op jit(solution)/shard_map/ppermute | solution.py:254
  24.9 36.9 %collective-permute-start.5 = (bf16[384,256]{1,0:T(8,128)(2,1)S(1)}, bf16[384,256]{1,0:T(8,128)(2,1)S(1)}, u32[]{:S(2)}, u32[]{:S(2)}) collective-permute-start(bf16[384,256]{1,0:T(8,128)(2,1)S(1)} %get-tuple-element.38), channel_id=1, source_target_pairs={{0,16},{1,19},{2,18},{3,17},{4,20},{5,23},{6,22},{7,21},{8,24},{9,... | collective-permute-start | bytes 589832 | tf_op jit(solution)/shard_map/ppermute | solution.py:254
  27.5 34.3 %collective-permute-start.6 = (bf16[384,256]{1,0:T(8,128)(2,1)S(1)}, bf16[384,256]{1,0:T(8,128)(2,1)S(1)}, u32[]{:S(2)}, u32[]{:S(2)}) collective-permute-start(bf16[384,256]{1,0:T(8,128)(2,1)S(1)} %get-tuple-element.39), channel_id=1, source_target_pairs={{0,20},{1,23},{2,22},{3,21},{4,16},{5,19},{6,18},{7,17},{8,28},{9,... | collective-permute-start | bytes 589832 | tf_op jit(solution)/shard_map/ppermute | solution.py:254
  29.0 0.6 copy-start.9
  31.6 17.8 %all-to-all-start.1 = ((f32[32,1,512]{2,1,0:T(1,128)}), f32[32,1,512]{2,1,0:T(1,128)S(1)}, u32[]{:S(2)}, u32[]{:S(2)}) async-start(f32[32,1,512]{2,1,0:T(1,128)} %get-tuple-element.30), calls=%async_computation.1 | async-start | bytes 131072 | tf_op jit(solution)/shard_map/all_to_all | solution.py:285
  49.4 0.6 copy-start.8
  52.1 24.3 %all-to-all-start.2 = ((f32[32,1,1792]{2,1,0:T(1,128)}), f32[32,1,1792]{2,1,0:T(1,128)S(1)}, u32[]{:S(2)}, u32[]{:S(2)}) async-start(f32[32,1,1792]{2,1,0:T(1,128)} %get-tuple-element.31), calls=%async_computation.2 | async-start | bytes 458752 | tf_op jit(solution)/shard_map/all_to_all | solution.py:295
  56.2 13.1 %collective-permute-start.7 = (bf16[384,256]{1,0:T(8,128)(2,1)S(1)}, bf16[384,256]{1,0:T(8,128)(2,1)S(1)}, u32[]{:S(2)}, u32[]{:S(2)}) collective-permute-start(bf16[384,256]{1,0:T(8,128)(2,1)S(1)} %get-tuple-element.40), channel_id=1, source_target_pairs={{0,24},{1,27},{2,26},{3,25},{4,28},{5,31},{6,30},{7,29},{8,16},{9,... | collective-permute-start | bytes 589832 | tf_op jit(solution)/shard_map/ppermute | solution.py:254
  59.8 14.3 %collective-permute-start.8 = (bf16[384,256]{1,0:T(8,128)(2,1)S(1)}, bf16[384,256]{1,0:T(8,128)(2,1)S(1)}, u32[]{:S(2)}, u32[]{:S(2)}) collective-permute-start(bf16[384,256]{1,0:T(8,128)(2,1)S(1)} %get-tuple-element.41), channel_id=1, source_target_pairs={{0,28},{1,31},{2,30},{3,29},{4,24},{5,27},{6,26},{7,25},{8,20},{9,... | collective-permute-start | bytes 589832 | tf_op jit(solution)/shard_map/ppermute | solution.py:254
  61.3 13.0 %collective-permute-start.9 = (bf16[384,256]{1,0:T(8,128)(2,1)S(1)}, bf16[384,256]{1,0:T(8,128)(2,1)S(1)}, u32[]{:S(2)}, u32[]{:S(2)}) collective-permute-start(bf16[384,256]{1,0:T(8,128)(2,1)S(1)} %collective-permute-done.1.refs_0_), channel_id=1, source_target_pairs={{0,1},{1,0},{2,3},{3,2},{4,5},{5,4},{6,7},{7,6},{8,9},{9,8},{10,11... | collective-permute-start | bytes 589832 | tf_op jit(solution)/shard_map/ppermute | solution.py:255
  61.8 12.9 %collective-permute-start.10 = (bf16[384,256]{1,0:T(8,128)(2,1)S(1)}, bf16[384,256]{1,0:T(8,128)(2,1)S(1)}, u32[]{:S(2)}, u32[]{:S(2)}) collective-permute-start(bf16[384,256]{1,0:T(8,128)(2,1)S(1)} %collective-permute-done.2.refs_1_), channel_id=1, source_target_pairs={{0,1},{1,0},{2,3},{3,2},{4,5},{5,4},{6,7},{7,6},{8,9},{9,8},{10,11... | collective-permute-start | bytes 589832 | tf_op jit(solution)/shard_map/ppermute | solution.py:255
  61.8 13.0 %collective-permute-start.11 = (bf16[384,256]{1,0:T(8,128)(2,1)S(1)}, bf16[384,256]{1,0:T(8,128)(2,1)S(1)}, u32[]{:S(2)}, u32[]{:S(2)}) collective-permute-start(bf16[384,256]{1,0:T(8,128)(2,1)S(1)} %collective-permute-done.3.refs_2_), channel_id=1, source_target_pairs={{0,1},{1,0},{2,3},{3,2},{4,5},{5,4},{6,7},{7,6},{8,9},{9,8},{10,11... | collective-permute-start | bytes 589832 | tf_op jit(solution)/shard_map/ppermute | solution.py:255
  69.2 6.0 %collective-permute-start.12 = (bf16[384,256]{1,0:T(8,128)(2,1)S(1)}, bf16[384,256]{1,0:T(8,128)(2,1)S(1)}, u32[]{:S(2)}, u32[]{:S(2)}) collective-permute-start(bf16[384,256]{1,0:T(8,128)(2,1)S(1)} %collective-permute-done.4.refs_3_), channel_id=1, source_target_pairs={{0,1},{1,0},{2,3},{3,2},{4,5},{5,4},{6,7},{7,6},{8,9},{9,8},{10,11... | collective-permute-start | bytes 589832 | tf_op jit(solution)/shard_map/ppermute | solution.py:255
  74.2 1.4 %collective-permute-start.13 = (bf16[384,256]{1,0:T(8,128)(2,1)S(1)}, bf16[384,256]{1,0:T(8,128)(2,1)S(1)}, u32[]{:S(2)}, u32[]{:S(2)}) collective-permute-start(bf16[384,256]{1,0:T(8,128)(2,1)S(1)} %collective-permute-done.5.refs_4_), channel_id=1, source_target_pairs={{0,1},{1,0},{2,3},{3,2},{4,5},{5,4},{6,7},{7,6},{8,9},{9,8},{10,11... | collective-permute-start | bytes 589832 | tf_op jit(solution)/shard_map/ppermute | solution.py:255
  74.3 1.6 %collective-permute-start.14 = (bf16[384,256]{1,0:T(8,128)(2,1)S(1)}, bf16[384,256]{1,0:T(8,128)(2,1)S(1)}, u32[]{:S(2)}, u32[]{:S(2)}) collective-permute-start(bf16[384,256]{1,0:T(8,128)(2,1)S(1)} %collective-permute-done.6.refs_5_), channel_id=1, source_target_pairs={{0,1},{1,0},{2,3},{3,2},{4,5},{5,4},{6,7},{7,6},{8,9},{9,8},{10,11... | collective-permute-start | bytes 589832 | tf_op jit(solution)/shard_map/ppermute | solution.py:255
  74.7 1.5 %collective-permute-start.15 = (bf16[384,256]{1,0:T(8,128)(2,1)S(1)}, bf16[384,256]{1,0:T(8,128)(2,1)S(1)}, u32[]{:S(2)}, u32[]{:S(2)}) collective-permute-start(bf16[384,256]{1,0:T(8,128)(2,1)S(1)} %collective-permute-done.7.refs_6_), channel_id=1, source_target_pairs={{0,1},{1,0},{2,3},{3,2},{4,5},{5,4},{6,7},{7,6},{8,9},{9,8},{10,11... | collective-permute-start | bytes 589832 | tf_op jit(solution)/shard_map/ppermute | solution.py:255
  74.8 1.6 %collective-permute-start.16 = (bf16[384,256]{1,0:T(8,128)(2,1)S(1)}, bf16[384,256]{1,0:T(8,128)(2,1)S(1)}, u32[]{:S(2)}, u32[]{:S(2)}) collective-permute-start(bf16[384,256]{1,0:T(8,128)(2,1)S(1)} %collective-permute-done.8.refs_7_), channel_id=1, source_target_pairs={{0,1},{1,0},{2,3},{3,2},{4,5},{5,4},{6,7},{7,6},{8,9},{9,8},{10,11... | collective-permute-start | bytes 589832 | tf_op jit(solution)/shard_map/ppermute | solution.py:255
  76.4 0.9 copy-start.4
  77.3 0.7 copy-start.7
  80.4 13.1 %collective-permute-start.20 = (bf16[256,256]{1,0:T(8,128)(2,1)S(1)}, bf16[256,256]{1,0:T(8,128)(2,1)S(1)}, u32[]{:S(2)}, u32[]{:S(2)}) collective-permute-start(bf16[256,256]{1,0:T(8,128)(2,1)S(1)} %get-tuple-element.45.refs_0_), channel_id=1, source_target_pairs={{0,24},{1,25},{2,26},{3,27},{4,28},{5,29},{6,30},{7,31},{8,0},{9,1... | collective-permute-start | bytes 393224 | tf_op jit(solution)/shard_map/ppermute | solution.py:154
  80.7 16.9 %collective-permute-start.19 = (bf16[256,256]{1,0:T(8,128)(2,1)S(1)}, bf16[256,256]{1,0:T(8,128)(2,1)S(1)}, u32[]{:S(2)}, u32[]{:S(2)}) collective-permute-start(bf16[256,256]{1,0:T(8,128)(2,1)S(1)} %get-tuple-element.45.refs_0_), channel_id=1, source_target_pairs={{0,8},{1,9},{2,10},{3,11},{4,12},{5,13},{6,14},{7,15},{8,16},{9,17... | collective-permute-start | bytes 393224 | tf_op jit(solution)/shard_map/ppermute | solution.py:154
  97.6 6.4 %collective-permute-start.21 = (bf16[2,256,256]{2,1,0:T(8,128)(2,1)S(1)}, bf16[2,256,256]{2,1,0:T(8,128)(2,1)S(1)}, u32[]{:S(2)}, u32[]{:S(2)}) collective-permute-start(bf16[2,256,256]{2,1,0:T(8,128)(2,1)S(1)} %pad_maximum_fusion.2), channel_id=1, source_target_pairs={{0,2},{1,5},{2,0},{3,7},{4,6},{5,1},{6,4},{7,3},{8,10},{9,13},{10,... | collective-permute-start | bytes 786440 | tf_op jit(solution)/shard_map/ppermute | solution.py:154
  98.8 8.9 %collective-permute-start.17 = (bf16[1,256,256]{2,1,0:T(8,128)(2,1)S(1)}, bf16[1,256,256]{2,1,0:T(8,128)(2,1)S(1)}, u32[]{:S(2)}, u32[]{:S(2)}) collective-permute-start(bf16[1,256,256]{2,1,0:T(8,128)(2,1)S(1)} %bitcast.48), channel_id=1, source_target_pairs={{0,2},{1,5},{2,0},{3,7},{4,6},{5,1},{6,4},{7,3},{8,10},{9,13},{10,... | collective-permute-start | bytes 393224 | tf_op jit(solution)/shard_map/ppermute | solution.py:154
  99.7 6.8 %collective-permute-start.23 = (bf16[256,256]{1,0:T(8,128)(2,1)S(1)}, bf16[256,256]{1,0:T(8,128)(2,1)S(1)}, u32[]{:S(2)}, u32[]{:S(2)}) collective-permute-start(bf16[256,256]{1,0:T(8,128)(2,1)S(1)} %broadcast_select_fusion), channel_id=1, source_target_pairs={{0,8},{1,25},{2,10},{3,27},{4,12},{5,29},{6,14},{7,31},{8,16},{9,1... | collective-permute-start | bytes 393224 | tf_op jit(solution)/shard_map/ppermute | solution.py:154
  104.1 15.3 %collective-permute-start.22 = (bf16[4,256,256]{2,1,0:T(8,128)(2,1)S(1)}, bf16[4,256,256]{2,1,0:T(8,128)(2,1)S(1)}, u32[]{:S(2)}, u32[]{:S(2)}) collective-permute-start(bf16[4,256,256]{2,1,0:T(8,128)(2,1)S(1)} %pad_maximum_fusion), channel_id=1, source_target_pairs={{0,4},{1,3},{2,6},{3,1},{4,0},{5,7},{6,2},{7,5},{8,12},{9,11},{10,... | collective-permute-start | bytes 1572872 | tf_op jit(solution)/shard_map/ppermute | solution.py:154
  106.5 6.4 %collective-permute-start.24 = (bf16[1,256,256]{2,1,0:T(8,128)(2,1)S(1)}, bf16[1,256,256]{2,1,0:T(8,128)(2,1)S(1)}, u32[]{:S(2)}, u32[]{:S(2)}) collective-permute-start(bf16[1,256,256]{2,1,0:T(8,128)(2,1)S(1)} %bitcast.50), channel_id=1, source_target_pairs={{0,2},{1,5},{2,0},{3,7},{4,6},{5,1},{6,4},{7,3},{8,10},{9,13},{10,... | collective-permute-start | bytes 393224 | tf_op jit(solution)/shard_map/ppermute | solution.py:154
  107.7 8.4 %collective-permute-start.18 = (bf16[2,256,256]{2,1,0:T(8,128)(2,1)S(1)}, bf16[2,256,256]{2,1,0:T(8,128)(2,1)S(1)}, u32[]{:S(2)}, u32[]{:S(2)}) collective-permute-start(bf16[2,256,256]{2,1,0:T(8,128)(2,1)S(1)} %pad_maximum_fusion.1), channel_id=1, source_target_pairs={{0,4},{1,3},{2,6},{3,1},{4,0},{5,7},{6,2},{7,5},{8,12},{9,11},{10,... | collective-permute-start | bytes 786440 | tf_op jit(solution)/shard_map/ppermute | solution.py:154
  113.0 6.4 %collective-permute-start.25 = (bf16[2,256,256]{2,1,0:T(8,128)(2,1)S(1)}, bf16[2,256,256]{2,1,0:T(8,128)(2,1)S(1)}, u32[]{:S(2)}, u32[]{:S(2)}) collective-permute-start(bf16[2,256,256]{2,1,0:T(8,128)(2,1)S(1)} %pad_maximum_fusion.3), channel_id=1, source_target_pairs={{0,4},{1,3},{2,6},{3,1},{4,0},{5,7},{6,2},{7,5},{8,12},{9,11},{10,... | collective-permute-start | bytes 786440 | tf_op jit(solution)/shard_map/ppermute | solution.py:154

commit v3 on v2

v3 whole, which is shorter than its diff:
```python
import functools

import jax
import jax.numpy as jnp
from jax import lax
from jax.experimental import pallas as pl
from jax.experimental.pallas import tpu as pltpu
from jax.sharding import PartitionSpec as P

ROUNDS = 3

lowest = -1e30
far = 1073741824.0
VMEM = pl.BlockSpec(memory_space=pltpu.VMEM)
SMEM = pl.BlockSpec(memory_space=pltpu.SMEM)
ANY = pl.BlockSpec(memory_space=pl.ANY)


def room(mebibytes):
    return pltpu.CompilerParams(vmem_limit_bytes=mebibytes * 1024 * 1024)


def opening(chunks, place, tokens, centroids, prices, kept, sent, mine, *refs):
    parcels, (tok, cen, acc, sem) = refs[:-4], refs[-4:]
    rows, cols = kept.shape[0], mine.shape[1]
    step = tok.shape[1] // chunks
    copies = []
    for i in range(chunks):
        part = pl.ds(i * step, step)
        copies.append((
            pltpu.make_async_copy(tokens.at[:, part], tok.at[:, part], sem.at[0, i]),
            pltpu.make_async_copy(centroids.at[:, part], cen.at[:, part], sem.at[1, i]),
        ))
    for pair in copies:
        pair[0].start()
        pair[1].start()
    for i, pair in enumerate(copies):
        pair[0].wait()
        pair[1].wait()
        part = slice(i * step, (i + 1) * step)
        product = lax.dot_general(
            tok[:, part], cen[:, part], (((1,), (1,)), ((), ())), preferred_element_type=jnp.float32
        )
        if i:
            acc[...] += product
        else:
            acc[...] = product
    for out, at in ((sent, 1), (kept, 0)):
        row = pl.multiple_of(place[at] * rows, rows)
        out[...] = acc[pl.ds(row, rows), :] * 0.015625 - prices[...]
    mine[...] = cen[:, pl.ds(pl.multiple_of(place[2] * cols, cols), cols)]
    for k, parcel in enumerate(parcels):
        parcel[...] = tok[:, pl.ds(pl.multiple_of(place[3 + k] * cols, cols), cols)]


def choose(values, eps):
    ids = lax.broadcasted_iota(jnp.int32, values.shape, 1).astype(jnp.float32)
    top = jnp.max(values, axis=1, keepdims=True)
    choice = jnp.min(jnp.where(values == top, ids, far), axis=1, keepdims=True)
    claims = ids == choice
    second = jnp.max(jnp.where(claims, lowest, values), axis=1, keepdims=True)
    bids = jnp.where(claims, top - second + eps, -1.0)
    return choice, claims, bids, jnp.max(bids, axis=0, keepdims=True)


def first_round(place, kept, theirs, epsilon, values, out):
    if theirs is None:
        values[...] = kept[...]
    else:
        own = kept.shape[1]
        swapped = place[0] != 0
        values[:, :own] = jnp.where(swapped, theirs[...], kept[...])
        values[:, own:] = jnp.where(swapped, kept[...], theirs[...])
    raised = choose(values[...], epsilon[0])[-1]
    out[...] = jnp.broadcast_to(raised[None], out.shape)


def first_round_whole(place, kept, epsilon, values, out):
    first_round(place, kept, None, epsilon, values, out)


def next_round(values, before, epsilon, bids, out, after):
    total = before[...] + jnp.maximum(jnp.max(bids[...], axis=0), 0.0)
    after[...] = total
    raised = choose(values[...] - total, epsilon[0])[-1]
    out[...] = jnp.broadcast_to(raised[None], out.shape)


def last_round(values, before, epsilon, bids, base, largest, out, after):
    rows, experts = values.shape
    total = before[...] + jnp.maximum(jnp.max(bids[...], axis=0), 0.0)
    after[...] = total
    choice, claims, spread, raised = choose(values[...] - total, epsilon[0])
    token = (base[0] + lax.broadcasted_iota(jnp.int32, (rows, experts), 0)).astype(jnp.float32)
    first = jnp.min(jnp.where(claims & (spread == raised), token, far), axis=0, keepdims=True)
    count = jnp.sum(claims.astype(jnp.float32), axis=0, keepdims=True)
    wide = out.shape[2] - 3 * experts
    lane = lax.broadcasted_iota(jnp.int32, (rows, wide), 1)
    row = lax.broadcasted_iota(jnp.int32, (rows, wide), 0)
    turned = jnp.sum(jnp.where(lane == row, choice, 0.0), axis=0, keepdims=True)
    turned = jnp.where(lane[:1] == rows, largest[0], turned)
    line = jnp.concatenate([raised, first, count, turned], axis=1)
    out[...] = jnp.broadcast_to(line[None], out.shape)


def finish(ne, rows, outer, place, info, before, prices, *refs):
    columns, (final, holder, best, counts_out, fits, *sums) = refs[: -5 - 2], refs[-5 - 2 :]
    experts = before.shape[1]
    own = prices.shape[1]
    start = place[0]
    if own % 128 == 0:
        start = pl.multiple_of(start, 128)
        raised = info[:, :, pl.ds(start, own)]
        firsts = info[:, :, pl.ds(pl.multiple_of(experts + start, 128), own)]
        earlier = before[:, pl.ds(start, own)]
        top_bid = jnp.max(raised, axis=0)
        first = jnp.min(jnp.where(raised == top_bid[None], firsts, far), axis=0)
        final[...] = prices[...] + earlier + jnp.maximum(top_bid, 0.0)
        holder[...] = jnp.where(top_bid > 0, first, -1.0).astype(jnp.int32)
    else:
        raised = info[:, :, :experts]
        top_bid = jnp.max(raised, axis=0)
        firsts = jnp.where(raised == top_bid[None], info[:, :, experts : 2 * experts], far)
        final[...] = before[...] + jnp.maximum(top_bid, 0.0)
        holder[...] = jnp.where(top_bid > 0, jnp.min(firsts, axis=0), -1.0).astype(jnp.int32)
    at = 3 * experts
    for c in range(ne):
        best[c] = info[place[1] * ne + c, :, at : at + rows].astype(jnp.int32)
    ids = (start + lax.broadcasted_iota(jnp.int32, (own, rows), 0)).astype(jnp.float32)
    total = jnp.zeros((own, sums[0].shape[1]), jnp.float32)
    for k, features in enumerate(columns):
        for c in range(ne):
            chosen = info[place[2 + k] * ne + c, :, at : at + rows]
            hot = jnp.where(ids == chosen, 1.0, 0.0).astype(jnp.bfloat16)
            total += jnp.dot(
                hot, features[c * rows : (c + 1) * rows, :], preferred_element_type=jnp.float32
            )
    part = own // len(sums)
    for i, out in enumerate(sums):
        out[...] = total[i * part : (i + 1) * part]
    share = info.shape[0] // outer
    parts = [
        jnp.sum(info[i * share : (i + 1) * share, :, 2 * experts : at], axis=0) for i in range(outer)
    ]
    largest = jnp.max(info[:, :, at + rows : at + rows + 1])
    fullest = jnp.max(functools.reduce(jnp.maximum, parts))
    fits[0] = jnp.where(fullest * largest <= 256.0, 1, 0)
    counts = functools.reduce(jnp.add, parts)
    expert_row = place[0] + lax.broadcasted_iota(jnp.int32, (own, experts), 0)
    lane = lax.broadcasted_iota(jnp.int32, (own, experts), 1)
    counts = jnp.sum(jnp.where(expert_row == lane, counts, 0.0), axis=1, keepdims=True)
    counts_out[...] = jnp.broadcast_to(jnp.maximum(counts, 1.0), counts_out.shape)


def blend(row, centroids, counts, *refs):
    sums, out = refs[:-1], refs[-1]
    rows, cols = out.shape
    total = functools.reduce(jnp.add, [s[...].astype(jnp.float32) for s in sums])
    old = centroids[row : row + rows, :].astype(jnp.float32)
    share = counts[row : row + rows, :1]
    out[...] = (0.5 * old + 0.5 * total / share).astype(out.dtype)


def assemble(plan, base, *refs):
    pieces, out, sem = refs[:-2], refs[-2], refs[-1]
    rows, cols = pieces[0].shape[-2:]
    copies = []
    for piece, (row, slots) in zip(pieces, plan):
        for i, slot in enumerate(slots):
            col = pl.multiple_of(base[slot] * cols, cols)
            source = piece if len(piece.shape) == 2 else piece.at[i]
            copies.append(
                pltpu.make_async_copy(
                    source, out.at[pl.ds(row, rows), pl.ds(col, cols)], sem.at[len(copies)]
                )
            )
    for copy in copies:
        copy.start()
    for copy in copies:
        copy.wait()


TURNS = ((0, 1), (2, 1))


def spread_out(dp, inner, wide, sums, mine, counts):
    bits = inner.bit_length() - 1
    member = lax.axis_index("dp") % inner
    core = lax.axis_index("expert")

    def move(value, masks):
        pairs = [(i * 2 + c, (i ^ masks[c]) * 2 + c) for i in range(dp) for c in range(2)]
        return lax.ppermute(value, ("dp", "expert"), pairs)

    parts = len(sums)
    rows, cols = sums[0].shape
    sent = [s if wide else s.astype(jnp.bfloat16) for s in sums]
    other = [move(s, (inner, inner)) for s in sent] if inner < dp else None
    held, pieces, plan, slots = [], [], [], []
    for p in range(parts):
        terms = [sums[p], other[p]] if other else [sums[p]]
        fresh = pl.pallas_call(
            functools.partial(blend, p * rows),
            out_shape=jax.ShapeDtypeStruct((rows, cols), mine.dtype),
            in_specs=[VMEM] * (2 + len(terms)),
            out_specs=VMEM,
            compiler_params=room(4),
            name="blend",
        )(mine, counts, *terms)
        held.append([(fresh[None], [(0, 0)])])
    for stage in range(bits):
        for p in range(parts):
            turns = [(stage + t) % bits for t in TURNS[p]]
            masks = [1 << t for t in turns]
            values = [v for v, _ in held[p]]
            where = [m for _, ms in held[p] for m in ms]
            value = values[0] if len(values) == 1 else jnp.concatenate(values)
            held[p].append((move(value, masks), [(a ^ masks[0], b ^ masks[1]) for a, b in where]))
    for p in range(parts):
        for value, where in held[p]:
            pieces.append(value)
            plan.append((p * rows, [len(slots) + i for i in range(len(where))]))
            slots += where
    base = jnp.stack([member ^ jnp.where(core == 0, a, b) for a, b in slots]).astype(jnp.int32)
    return pl.pallas_call(
        functools.partial(assemble, plan),
        out_shape=jax.ShapeDtypeStruct((parts * rows, inner * cols), mine.dtype),
        in_specs=[SMEM] + [VMEM] * len(pieces),
        out_specs=ANY,
        scratch_shapes=[pltpu.SemaphoreType.DMA((len(slots),))],
        compiler_params=room(16),
        name="assemble",
    )(base, *pieces)


def body(dp, ne, tokens, centroids, prices, epsilon):
    f32 = jnp.float32
    local_tokens, width = tokens.shape
    own = centroids.shape[0]
    experts = own * ne
    devices = dp * ne
    rows = local_tokens // ne
    cols = width // dp
    dp_at, expert_at = lax.axis_index("dp"), lax.axis_index("expert")
    everywhere = ("dp", "expert")
    outer = 2 if ne == 2 and dp % 16 == 0 and dp & (dp - 1) == 0 else 1
    inner = dp // outer
    cols = width // inner
    paired = outer == 2 and cols % 128 == 0 and own % 32 == 0
    swap = [(0, 1), (1, 0)]

    def shape(*sizes, dtype=f32):
        return jax.ShapeDtypeStruct(sizes, dtype)

    line, spread = shape(1, experts), shape(devices, 1, experts)
    at = jnp.stack([expert_at]).astype(jnp.int32)
    if paired:
        half = inner // 2
        chunks = 4
        theirs = [dp_at ^ (2 * k + expert_at) for k in range(half)]
        place = [expert_at, 1 - expert_at, dp_at % inner] + [t % inner for t in theirs]
        place = jnp.stack(place).astype(jnp.int32)
        kept, sent, mine, *parcels = pl.pallas_call(
            functools.partial(opening, chunks),
            out_shape=[shape(rows, own)] * 2
            + [shape(own, cols, dtype=centroids.dtype)]
            + [shape(local_tokens, cols, dtype=tokens.dtype)] * half,
            in_specs=[SMEM, ANY, ANY, VMEM],
            out_specs=[VMEM] * (3 + half),
            scratch_shapes=[
                pltpu.VMEM(tokens.shape, tokens.dtype),
                pltpu.VMEM(centroids.shape, centroids.dtype),
                pltpu.VMEM((local_tokens, own), f32),
                pltpu.SemaphoreType.DMA((2, chunks)),
            ],
            compiler_params=room(48),
            name="opening",
        )(place, tokens, centroids, prices.reshape(1, own))
        received = lax.ppermute(sent, "expert", swap)
        values, bids = pl.pallas_call(
            first_round,
            out_shape=(shape(rows, experts), spread),
            in_specs=[SMEM, VMEM, VMEM, SMEM],
            out_specs=(VMEM, VMEM),
            compiler_params=room(4),
            name="first_round",
        )(at, kept, received, epsilon)
        columns = []
        for k, parcel in enumerate(parcels):
            pairs = [
                (i * 2 + c, (i ^ (2 * k + c)) * 2 + c) for i in range(dp) for c in range(2)
            ]
            columns.append(lax.ppermute(parcel, everywhere, pairs))
        columns += [lax.ppermute(c, "expert", swap) for c in columns]
        sources = theirs + [dp_at ^ (2 * k + 1 - expert_at) for k in range(half)]
    else:
        parcels = tokens.reshape(local_tokens, dp, cols).transpose(1, 0, 2)
        columns = lax.all_to_all(parcels, "dp", 0, 0, tiled=True)
        columns = [columns.reshape(dp * local_tokens, cols)[i * local_tokens :][:local_tokens] for i in range(dp)]
        sources = list(range(dp))
        mine = lax.dynamic_slice_in_dim(centroids, dp_at * cols, cols, 1)
        part = lax.dot_general(
            tokens, centroids, (((1,), (1,)), ((), ())), preferred_element_type=f32
        ) * 0.015625 - prices
        part = lax.all_to_all(part, "expert", 0, 1, tiled=True)
        values, bids = pl.pallas_call(
            first_round_whole,
            out_shape=(shape(rows, experts), spread),
            in_specs=[SMEM, VMEM, SMEM],
            out_specs=(VMEM, VMEM),
            compiler_params=room(4),
            name="first_round",
        )(at, part, epsilon)

    total = jnp.zeros((1, experts), f32)
    for _ in range(ROUNDS - 2):
        bids = lax.all_to_all(bids, everywhere, 0, 0, tiled=True)
        bids, total = pl.pallas_call(
            next_round,
            out_shape=(spread, line),
            in_specs=[VMEM, VMEM, SMEM, VMEM],
            out_specs=(VMEM, VMEM),
            compiler_params=room(4),
            name="next_round",
        )(values, total, epsilon, bids)
    bids = lax.all_to_all(bids, everywhere, 0, 0, tiled=True)
    wide = (rows // 128 + 1) * 128
    largest = jnp.max(jnp.abs(tokens)).astype(f32).reshape(1)
    base = (dp_at * local_tokens + expert_at * rows).astype(jnp.int32).reshape(1)
    info, total = pl.pallas_call(
        last_round,
        out_shape=(shape(devices, 1, 3 * experts + wide), line),
        in_specs=[VMEM, VMEM, SMEM, VMEM, SMEM, SMEM],
        out_specs=(VMEM, VMEM),
        compiler_params=room(8),
        name="last_round",
    )(values, total, epsilon, bids, base, largest)
    info = lax.all_to_all(info, everywhere, 0, 0, tiled=True)

    place = jnp.stack([expert_at * own, dp_at] + sources).astype(jnp.int32)
    direct = own % 128 == 0
    listed = own if direct else experts
    final, holder, best, counts, fits, *sums = pl.pallas_call(
        functools.partial(finish, ne, rows, outer),
        out_shape=(
            shape(1, listed),
            shape(1, listed, dtype=jnp.int32),
            shape(ne, 1, rows, dtype=jnp.int32),
            shape(own, 128),
            shape(1, dtype=jnp.int32),
        )
        + (shape(own // 2, cols),) * 2,
        in_specs=[SMEM] + [VMEM] * (3 + len(columns)),
        out_specs=(VMEM, VMEM, VMEM, VMEM, SMEM, VMEM, VMEM),
        compiler_params=room(16),
        name="finish",
    )(place, info, total, prices.reshape(1, own), *columns)
    if paired:
        spread_as = [functools.partial(spread_out, dp, inner, wide) for wide in (True, False)]
        refreshed = lax.cond(fits[0] > 0, spread_as[1], spread_as[0], sums, mine, counts)
    else:
        sums = jnp.concatenate(sums)
        fresh = 0.5 * mine.astype(f32) + 0.5 * sums / counts[:, :1]
        refreshed = lax.all_gather(fresh.astype(centroids.dtype), "dp", axis=1, tiled=True)
    if direct:
        final, holder = final[0], holder[0]
    else:
        final = prices + lax.dynamic_slice_in_dim(final[0], expert_at * own, own, 0)
        holder = lax.dynamic_slice_in_dim(holder[0], expert_at * own, own, 0)
    return final, best.reshape(local_tokens), holder, refreshed


def solution(mesh):
    placed = (P("dp", None), P("expert", None), P("expert"), P())
    return jax.shard_map(
        functools.partial(body, mesh.shape["dp"], mesh.shape["expert"]),
        mesh=mesh,
        in_specs=placed,
        out_specs=(P("expert"), P("dp"), P("expert"), P("expert", None)),
        check_vma=False,
    )
```

time: 122 us -> 119 us (0.975)
  starting transfers between devices: 47.5 us -> 30.1 us
  waiting for transfers between devices: 49.9 us -> 64.3 us
  local copies, waits for them, and re-layouts: 9.92 us -> 3.2 us
  other arithmetic: 0.17 us -> 3.12 us
  Pallas kernels: 12.5 us -> 14.5 us
  between operations: 1.46 us -> 2.7 us
    ppermute x9 -> x8, waiting for transfers between devices: 23.8 us -> 42.2 us  [move(): return lax.ppermute(value, ('dp', 'expert'), pairs)]
    ppermute x8 -> x4, waiting for transfers between devices: 11.9 us -> 0.01 us  [body(): columns.append(lax.ppermute(parcel, everywhere, pairs))]
    ppermute x8 -> x4, starting transfers between devices: 13.4 us -> 5.14 us  [body(): columns.append(lax.ppermute(parcel, everywhere, pairs))]
    ppermute x9 -> x8, starting transfers between devices: 14.3 us -> 7.25 us  [move(): return lax.ppermute(value, ('dp', 'expert'), pairs)]
    all_to_all x1, waiting for transfers between devices: 0.01 us -> 6.33 us  [body(): info = lax.all_to_all(info, everywhere, 0, 0, tiled=True)]
    unnamed x22 -> x6, local copies, waits for them, and re-layouts: 8.39 us -> 2.27 us
    pallas_call x3 -> x5, Pallas kernels: 6.49 us -> 11.5 us  [the longest x1 4.74 us: body(): pl.pallas_call(functools.partial(opening, chunks), out_shape=[shape(rows,...]
    reduce_max x0 -> x1, other arithmetic: none -> 2.94 us  [body(): largest = jnp.max(jnp.abs(tokens)).astype(f32).reshape(1)]
  transfers between devices with their start and end apart: 29 -> 20, of which waited for: 14 -> 14; matrix products, arithmetic and copies ran while one was open for 1% -> 3% of each run, Pallas kernels for 5% -> 4%
where the time goes in v3:
time: 119 us; the launch traced here: 118 us
  waiting for transfers between devices  64.3 us (54%)
  starting transfers between devices  30.1 us (25%)
  Pallas kernels  14.5 us (12%)
  local copies, waits for them, and re-layouts  3.2 us (3%)
  other arithmetic  3.12 us (3%)
  between operations  2.7 us (2%)
    ppermute x8, waiting for transfers between devices, move(): return lax.ppermute(value, ('dp', 'expert'), pairs)  42.2 us
    all_to_all x2, waiting for transfers between devices, body(): bids = lax.all_to_all(bids, everywhere, 0, 0, tiled=True)  13.1 us
    all_to_all x2, starting transfers between devices, body(): bids = lax.all_to_all(bids, everywhere, 0, 0, tiled=True)  12 us
    ppermute x8, starting transfers between devices, move(): return lax.ppermute(value, ('dp', 'expert'), pairs)  7.25 us
    all_to_all x1, waiting for transfers between devices, body(): info = lax.all_to_all(info, everywhere, 0, 0, tiled=True)  6.33 us
    ppermute x4, starting transfers between devices, body(): columns.append(lax.ppermute(parcel, everywhere, pairs))  5.14 us
    pallas_call x1, Pallas kernels, body(): pl.pallas_call(functools.partial(opening, chunks), out_shape=[shape(rows,...  4.74 us
    all_to_all x1, starting transfers between devices, body(): info = lax.all_to_all(info, everywhere, 0, 0, tiled=True)  4.11 us
  transfers between devices with their start and end apart: 20, of which 14 were waited for; matrix products, arithmetic and copies ran while one was open for 3% of the time, Pallas kernels for 4%

profile of v3, /device:TPU:0, one launch (start us, length us, event | category | flops | bytes accessed | tf_op | source)
XLA Modules:
  0.0 118.1 jit_solution(17484449634026175797)
XLA Ops:
  0.7 0.1 stack.170.place
  0.8 1.6 %copy-done = bf16[256,4096]{1,0:T(8,128)(2,1)S(1)} copy-done((bf16[256,4096]{1,0:T(8,128)(2,1)S(1)}, bf16[256,4096]{1,0:T(8,128)(2,1)}, u32[]{:S(2)}) %copy-start) | copy-done | bytes 2097176
  2.4 0.7 copy-done.1
  3.1 4.7 %opening.1 = (f32[192,256]{1,0:T(8,128)S(1)}, f32[192,256]{1,0:T(8,128)S(1)}, bf16[256,512]{1,0:T(8,128)(2,1)}, bf16[384,512]{1,0:T(8,128)(2,1)}, bf16[384,512]{...) custom-call(s32[7]{0:T(128)S(1)} %stack.170.place, bf16[384,4096]{1,0:T(8,128)(2,1)} %tokens.1, ...), custom_call_target="tpu_custom_call" | custom-call | tf_op jit(solution)/shard_map/opening/pallas_call | solution.py:263
  7.8 0.5 collective-permute-start.16
  9.0 0.4 collective-permute-done.16.theirs
  9.4 0.9 first_round.1
  10.3 7.2 %all-to-all-start = ((f32[32,1,512]{2,1,0:T(1,128)}), f32[32,1,512]{2,1,0:T(1,128)S(1)}, u32[]{:S(2)}, u32[]{:S(2)}) async-start(f32[32,1,512]{2,1,0:T(1,128)} %get-tuple-element.54), calls=%async_computation | async-start | bytes 131072 | tf_op jit(solution)/shard_map/all_to_all | solution.py:317
  17.6 1.7 %collective-permute-start.17 = (bf16[384,512]{1,0:T(8,128)(2,1)}, bf16[384,512]{1,0:T(8,128)(2,1)S(1)}, u32[]{:S(2)}, u32[]{:S(2)}) collective-permute-start(bf16[384,512]{1,0:T(8,128)(2,1)} %get-tuple-element.59), channel_id=1, source_target_pairs={{0,0},{1,3},{2,2},{3,1},{4,4},{5,7},{6,6},{7,5},{8,8},{9,11},{10,1... | collective-permute-start | bytes 1179656 | tf_op jit(solution)/shard_map/ppermute | solution.py:293
  19.2 1.8 %collective-permute-start.18 = (bf16[384,512]{1,0:T(8,128)(2,1)S(1)}, bf16[384,512]{1,0:T(8,128)(2,1)S(1)}, u32[]{:S(2)}, u32[]{:S(2)}) collective-permute-start(bf16[384,512]{1,0:T(8,128)(2,1)S(1)} %get-tuple-element.60), channel_id=1, source_target_pairs={{0,4},{1,7},{2,6},{3,5},{4,0},{5,3},{6,2},{7,1},{8,12},{9,15},{10,... | collective-permute-start | bytes 1179656 | tf_op jit(solution)/shard_map/ppermute | solution.py:293
  21.0 1.5 %collective-permute-start.19 = (bf16[384,512]{1,0:T(8,128)(2,1)S(1)}, bf16[384,512]{1,0:T(8,128)(2,1)S(1)}, u32[]{:S(2)}, u32[]{:S(2)}) collective-permute-start(bf16[384,512]{1,0:T(8,128)(2,1)S(1)} %get-tuple-element.61), channel_id=1, source_target_pairs={{0,8},{1,11},{2,10},{3,9},{4,12},{5,15},{6,14},{7,13},{8,0},{9,3},... | collective-permute-start | bytes 1179656 | tf_op jit(solution)/shard_map/ppermute | solution.py:293
  22.5 0.3 collective-permute-start.20
  22.7 2.4 %all-to-all-done.bids = f32[32,1,512]{2,1,0:T(1,128)S(1)} async-done(((f32[32,1,512]{2,1,0:T(1,128)}), f32[32,1,512]{2,1,0:T(1,128)S(1)}, u32[]{:S(2)}, u32[]{:S(2)}) %all-to-all-start) | async-done | bytes 65568 | tf_op jit(solution)/shard_map/all_to_all | solution.py:317
  25.1 0.9 next_round.1
  26.0 4.8 %all-to-all-start.1 = ((f32[32,1,512]{2,1,0:T(1,128)}), f32[32,1,512]{2,1,0:T(1,128)S(1)}, u32[]{:S(2)}, u32[]{:S(2)}) async-start(f32[32,1,512]{2,1,0:T(1,128)} %get-tuple-element.56), calls=%async_computation.1 | async-start | bytes 131072 | tf_op jit(solution)/shard_map/all_to_all | solution.py:326
  30.8 2.9 %abs_reduce_fusion = bf16[]{:T(256)} fusion(bf16[384,4096]{1,0:T(8,128)(2,1)} %tokens.1), kind=kLoop, calls=%fused_computation.8 | loop fusion | flops 3145727 | bytes 3145730 | tf_op jit(solution)/shard_map/reduce_max | solution.py:328
  34.4 10.7 %all-to-all-done.1.bids = f32[32,1,512]{2,1,0:T(1,128)S(1)} async-done(((f32[32,1,512]{2,1,0:T(1,128)}), f32[32,1,512]{2,1,0:T(1,128)S(1)}, u32[]{:S(2)}, u32[]{:S(2)}) %all-to-all-start.1) | async-done | bytes 65568 | tf_op jit(solution)/shard_map/all_to_all | solution.py:326
  45.1 1.1 last_round.1
  46.2 4.1 %all-to-all-start.2 = ((f32[32,1,1792]{2,1,0:T(1,128)}), f32[32,1,1792]{2,1,0:T(1,128)S(1)}, u32[]{:S(2)}, u32[]{:S(2)}) async-start(f32[32,1,1792]{2,1,0:T(1,128)} %get-tuple-element.57), calls=%async_computation.2 | async-start | bytes 458752 | tf_op jit(solution)/shard_map/all_to_all | solution.py:338
  50.3 0.3 collective-permute-start.21
  50.6 0.3 collective-permute-start.22
  50.9 0.3 collective-permute-start.23
  51.1 0.3 collective-permute-start.24
  51.4 0.1 stack.162.place
  51.5 0.6 collective-permute-done.21.refs_4_
  52.1 0.6 collective-permute-done.22.refs_5_
  52.6 0.6 collective-permute-done.23.refs_6_
  53.2 0.6 collective-permute-done.24.refs_7_
  53.8 6.3 %all-to-all-done.2.info = f32[32,1,1792]{2,1,0:T(1,128)S(1)} async-done(((f32[32,1,1792]{2,1,0:T(1,128)}), f32[32,1,1792]{2,1,0:T(1,128)S(1)}, u32[]{:S(2)}, u32[]{:S(2)}) %all-to-all-start.2) | async-done | bytes 229408 | tf_op jit(solution)/shard_map/all_to_all | solution.py:338
  60.1 2.5 %finish.1 = (f32[1,256]{1,0:T(1,128)}, s32[1,256]{1,0:T(1,128)}, s32[2,1,192]{2,1,0:T(1,128)S(1)}, f32[256,128]{1,0:T(8,128)S(1)}, s32[1]{0:T(128)}, /*index=5*/f32[128,512]{1,0:T(8,128)}, f32[128,512]{1,0:T(8,128)}) custom-call(s32[10]{0:T(128)S(1)} %stack.162.place, f32[32,1,1792]{2,1,0:T(1,128)S(1)} %all-to-all-done.2.info, ...), custom_call_target="tpu_custom_call" | custom-call | tf_op jit(solution)/shard_map/finish/pallas_call | solution.py:343
  63.3 0.7 reshape.31
  64.0 54.1 %conditional.1 = (bf16[256,4096]{1,0:T(8,128)(2,1)}) conditional(s32[]{:T(128)} %bitcast.54, (f32[128,512]{1,0:T(8,128)}, bf16[256,512]{1,0:T(8,128)(2,1)}, f32[256,128]{1,0:T(8,128)S(1)}, f32[128,512]{1,0:T(8,128)}) %tuple.14, (f32[128,512]{1,0:T(8,128)}, bf16[256,512]{1,0:T(8,128)(2,1)}, f32[256,128]{1,0:T(8,128)S(1)}, f32[128,512]{1,0:T(8,128)}) %tuple.14), branch_computations={%region_1.2_spmd, %region_2.3_spmd} | conditional | flops 1441834 | bytes 12583850 | solution.py:360
  64.0 0.6 collective-permute-start
  64.6 2.3 %collective-permute-start.4 = (f32[128,512]{1,0:T(8,128)}, f32[128,512]{1,0:T(8,128)S(1)}, u32[]{:S(2)}, u32[]{:S(2)}) collective-permute-start(f32[128,512]{1,0:T(8,128)} %get-tuple-element.22.refs_0_), channel_id=1, source_target_pairs={{0,16},{1,17},{2,18},{3,19},{4,20},{5,21},{6,22},{7,23},{8,24},{9,... | collective-permute-start | bytes 786440 | tf_op jit(solution)/shard_map/cond/branch_0_fun/ppermute | solution.py:193
  66.9 17.5 %collective-permute-done.refs_1_ = f32[128,512]{1,0:T(8,128)S(1)} collective-permute-done((f32[128,512]{1,0:T(8,128)}, f32[128,512]{1,0:T(8,128)S(1)}, u32[]{:S(2)}, u32[]{:S(2)}) %collective-permute-start) | collective-permute-done | bytes 262176 | tf_op jit(solution)/shard_map/cond/branch_0_fun/ppermute | solution.py:193
  84.4 1.1 blend.4
  85.5 1.3 %collective-permute-start.1 = (bf16[1,128,512]{2,1,0:T(8,128)(2,1)S(1)}, bf16[1,128,512]{2,1,0:T(8,128)(2,1)S(1)}, u32[]{:S(2)}, u32[]{:S(2)}) collective-permute-start(bf16[1,128,512]{2,1,0:T(8,128)(2,1)S(1)} %bitcast.64), channel_id=1, source_target_pairs={{0,2},{1,5},{2,0},{3,7},{4,6},{5,1},{6,4},{7,3},{8,10},{9,13},{10,... | collective-permute-start | bytes 393224 | tf_op jit(solution)/shard_map/cond/branch_0_fun/ppermute | solution.py:193
  86.8 3.1 %collective-permute-done.4.refs_1_ = f32[128,512]{1,0:T(8,128)S(1)} collective-permute-done((f32[128,512]{1,0:T(8,128)}, f32[128,512]{1,0:T(8,128)S(1)}, u32[]{:S(2)}, u32[]{:S(2)}) %collective-permute-start.4) | collective-permute-done | bytes 262176 | tf_op jit(solution)/shard_map/cond/branch_0_fun/ppermute | solution.py:193
  89.9 1.1 blend.5
  91.2 0.7 collective-permute-start.2
  91.9 5.6 %collective-permute-done.5.refs_5_ = bf16[1,128,512]{2,1,0:T(8,128)(2,1)S(1)} collective-permute-done((bf16[1,128,512]{2,1,0:T(8,128)(2,1)S(1)}, bf16[1,128,512]{2,1,0:T(8,128)(2,1)S(1)}, u32[]{:S(2)}, u32[]{:S(2)}) %collective-permute-start.5) | collective-permute-done | bytes 131104 | tf_op jit(solution)/shard_map/cond/branch_0_fun/ppermute | solution.py:193
  97.5 1.2 collective-permute-start.6
  98.8 1.0 collective-permute-start.3
  99.8 7.0 %collective-permute-done.6.refs_6_ = bf16[2,128,512]{2,1,0:T(8,128)(2,1)S(1)} collective-permute-done((bf16[2,128,512]{2,1,0:T(8,128)(2,1)S(1)}, bf16[2,128,512]{2,1,0:T(8,128)(2,1)S(1)}, u32[]{:S(2)}, u32[]{:S(2)}) %collective-permute-start.6) | collective-permute-done | bytes 262176 | tf_op jit(solution)/shard_map/cond/branch_0_fun/ppermute | solution.py:193
  107.0 0.1 stack.117.base
  107.0 1.0 collective-permute-done.3.refs_3_
  108.0 8.1 %collective-permute-done.7.refs_7_ = bf16[4,128,512]{2,1,0:T(8,128)(2,1)S(1)} collective-permute-done((bf16[4,128,512]{2,1,0:T(8,128)(2,1)S(1)}, bf16[4,128,512]{2,1,0:T(8,128)(2,1)S(1)}, u32[]{:S(2)}, u32[]{:S(2)}) %collective-permute-start.7) | collective-permute-done | bytes 524320 | tf_op jit(solution)/shard_map/cond/branch_0_fun/ppermute | solution.py:193
  116.1 2.0 %assemble.2 = bf16[256,4096]{1,0:T(8,128)(2,1)} custom-call(s32[16]{0:T(128)S(1)} %stack.117.base, bf16[1,128,512]{2,1,0:T(8,128)(2,1)S(1)} %bitcast.67, bf16[1,128,512]{2,1,0:T(8,128)(2,1)S(1)} %collective-permute-done.1.refs_1_, bf16[2,128,512]{2,1,0:T(8,128)(2,1)S(1)} %collective-permute-done.2.refs_2_, ...), custom_call_target="tpu_custom_call" | custom-call | tf_op jit(solution)/shard_map/cond/branch_0_fun/assemble/pallas_call | solution.py:225
  (18 shorter events, 0.3 us)
Async XLA Ops:
  0.8 1.6 %copy-start = (bf16[256,4096]{1,0:T(8,128)(2,1)S(1)}, bf16[256,4096]{1,0:T(8,128)(2,1)}, u32[]{:S(2)}) copy-start(bf16[256,4096]{1,0:T(8,128)(2,1)} %centroids.1) | copy-start | bytes 6291460
  2.4 0.7 copy-start.1
  7.8 1.6 %collective-permute-start.16 = (f32[192,256]{1,0:T(8,128)S(1)}, f32[192,256]{1,0:T(8,128)S(1)}, u32[]{:S(2)}, u32[]{:S(2)}) collective-permute-start(f32[192,256]{1,0:T(8,128)S(1)} %get-tuple-element.52), channel_id=1, source_target_pairs={{0,1},{1,0},{2,3},{3,2},{4,5},{5,4},{6,7},{7,6},{8,9},{9,8},{10,11... | collective-permute-start | bytes 589832 | tf_op jit(solution)/shard_map/ppermute | solution.py:279
  10.3 14.7 %all-to-all-start = ((f32[32,1,512]{2,1,0:T(1,128)}), f32[32,1,512]{2,1,0:T(1,128)S(1)}, u32[]{:S(2)}, u32[]{:S(2)}) async-start(f32[32,1,512]{2,1,0:T(1,128)} %get-tuple-element.54), calls=%async_computation | async-start | bytes 131072 | tf_op jit(solution)/shard_map/all_to_all | solution.py:317
  17.6 32.7 %collective-permute-start.17 = (bf16[384,512]{1,0:T(8,128)(2,1)}, bf16[384,512]{1,0:T(8,128)(2,1)S(1)}, u32[]{:S(2)}, u32[]{:S(2)}) collective-permute-start(bf16[384,512]{1,0:T(8,128)(2,1)} %get-tuple-element.59), channel_id=1, source_target_pairs={{0,0},{1,3},{2,2},{3,1},{4,4},{5,7},{6,6},{7,5},{8,8},{9,11},{10,1... | collective-permute-start | bytes 1179656 | tf_op jit(solution)/shard_map/ppermute | solution.py:293
  19.2 31.4 %collective-permute-start.18 = (bf16[384,512]{1,0:T(8,128)(2,1)S(1)}, bf16[384,512]{1,0:T(8,128)(2,1)S(1)}, u32[]{:S(2)}, u32[]{:S(2)}) collective-permute-start(bf16[384,512]{1,0:T(8,128)(2,1)S(1)} %get-tuple-element.60), channel_id=1, source_target_pairs={{0,4},{1,7},{2,6},{3,5},{4,0},{5,3},{6,2},{7,1},{8,12},{9,15},{10,... | collective-permute-start | bytes 1179656 | tf_op jit(solution)/shard_map/ppermute | solution.py:293
  21.0 29.9 %collective-permute-start.19 = (bf16[384,512]{1,0:T(8,128)(2,1)S(1)}, bf16[384,512]{1,0:T(8,128)(2,1)S(1)}, u32[]{:S(2)}, u32[]{:S(2)}) collective-permute-start(bf16[384,512]{1,0:T(8,128)(2,1)S(1)} %get-tuple-element.61), channel_id=1, source_target_pairs={{0,8},{1,11},{2,10},{3,9},{4,12},{5,15},{6,14},{7,13},{8,0},{9,3},... | collective-permute-start | bytes 1179656 | tf_op jit(solution)/shard_map/ppermute | solution.py:293
  22.5 28.7 %collective-permute-start.20 = (bf16[384,512]{1,0:T(8,128)(2,1)S(1)}, bf16[384,512]{1,0:T(8,128)(2,1)S(1)}, u32[]{:S(2)}, u32[]{:S(2)}) collective-permute-start(bf16[384,512]{1,0:T(8,128)(2,1)S(1)} %get-tuple-element.62), channel_id=1, source_target_pairs={{0,12},{1,15},{2,14},{3,13},{4,8},{5,11},{6,10},{7,9},{8,4},{9,7},... | collective-permute-start | bytes 1179656 | tf_op jit(solution)/shard_map/ppermute | solution.py:293
  26.0 34.1 %copy-start.2 = (f32[256]{0:T(256)S(1)}, f32[256]{0:T(256)}, u32[]{:S(2)}) copy-start(f32[256]{0:T(256)} %param.8) | copy-start | bytes 3076
  26.0 19.0 %all-to-all-start.1 = ((f32[32,1,512]{2,1,0:T(1,128)}), f32[32,1,512]{2,1,0:T(1,128)S(1)}, u32[]{:S(2)}, u32[]{:S(2)}) async-start(f32[32,1,512]{2,1,0:T(1,128)} %get-tuple-element.56), calls=%async_computation.1 | async-start | bytes 131072 | tf_op jit(solution)/shard_map/all_to_all | solution.py:326
  46.2 13.9 %all-to-all-start.2 = ((f32[32,1,1792]{2,1,0:T(1,128)}), f32[32,1,1792]{2,1,0:T(1,128)S(1)}, u32[]{:S(2)}, u32[]{:S(2)}) async-start(f32[32,1,1792]{2,1,0:T(1,128)} %get-tuple-element.57), calls=%async_computation.2 | async-start | bytes 458752 | tf_op jit(solution)/shard_map/all_to_all | solution.py:338
  50.3 1.8 %collective-permute-start.21 = (bf16[384,512]{1,0:T(8,128)(2,1)S(1)}, bf16[384,512]{1,0:T(8,128)(2,1)S(1)}, u32[]{:S(2)}, u32[]{:S(2)}) collective-permute-start(bf16[384,512]{1,0:T(8,128)(2,1)S(1)} %collective-permute-done.17.refs_0_), channel_id=1, source_target_pairs={{0,1},{1,0},{2,3},{3,2},{4,5},{5,4},{6,7},{7,6},{8,9},{9,8},{10,11... | collective-permute-start | bytes 1179656 | tf_op jit(solution)/shard_map/ppermute | solution.py:294
  50.6 2.0 %collective-permute-start.22 = (bf16[384,512]{1,0:T(8,128)(2,1)S(1)}, bf16[384,512]{1,0:T(8,128)(2,1)S(1)}, u32[]{:S(2)}, u32[]{:S(2)}) collective-permute-start(bf16[384,512]{1,0:T(8,128)(2,1)S(1)} %collective-permute-done.18.refs_1_), channel_id=1, source_target_pairs={{0,1},{1,0},{2,3},{3,2},{4,5},{5,4},{6,7},{7,6},{8,9},{9,8},{10,11... | collective-permute-start | bytes 1179656 | tf_op jit(solution)/shard_map/ppermute | solution.py:294
  50.9 2.3 %collective-permute-start.23 = (bf16[384,512]{1,0:T(8,128)(2,1)S(1)}, bf16[384,512]{1,0:T(8,128)(2,1)S(1)}, u32[]{:S(2)}, u32[]{:S(2)}) collective-permute-start(bf16[384,512]{1,0:T(8,128)(2,1)S(1)} %collective-permute-done.19.refs_2_), channel_id=1, source_target_pairs={{0,1},{1,0},{2,3},{3,2},{4,5},{5,4},{6,7},{7,6},{8,9},{9,8},{10,11... | collective-permute-start | bytes 1179656 | tf_op jit(solution)/shard_map/ppermute | solution.py:294
  51.1 2.6 %collective-permute-start.24 = (bf16[384,512]{1,0:T(8,128)(2,1)S(1)}, bf16[384,512]{1,0:T(8,128)(2,1)S(1)}, u32[]{:S(2)}, u32[]{:S(2)}) collective-permute-start(bf16[384,512]{1,0:T(8,128)(2,1)S(1)} %collective-permute-done.20.refs_3_), channel_id=1, source_target_pairs={{0,1},{1,0},{2,3},{3,2},{4,5},{5,4},{6,7},{7,6},{8,9},{9,8},{10,11... | collective-permute-start | bytes 1179656 | tf_op jit(solution)/shard_map/ppermute | solution.py:294
  64.0 20.4 %collective-permute-start = (f32[128,512]{1,0:T(8,128)}, f32[128,512]{1,0:T(8,128)S(1)}, u32[]{:S(2)}, u32[]{:S(2)}) collective-permute-start(f32[128,512]{1,0:T(8,128)} %get-tuple-element.21.refs_0_), channel_id=1, source_target_pairs={{0,16},{1,17},{2,18},{3,19},{4,20},{5,21},{6,22},{7,23},{8,24},{9,... | collective-permute-start | bytes 786440 | tf_op jit(solution)/shard_map/cond/branch_0_fun/ppermute | solution.py:193
  64.6 25.3 %collective-permute-start.4 = (f32[128,512]{1,0:T(8,128)}, f32[128,512]{1,0:T(8,128)S(1)}, u32[]{:S(2)}, u32[]{:S(2)}) collective-permute-start(f32[128,512]{1,0:T(8,128)} %get-tuple-element.22.refs_0_), channel_id=1, source_target_pairs={{0,16},{1,17},{2,18},{3,19},{4,20},{5,21},{6,22},{7,23},{8,24},{9,... | collective-permute-start | bytes 786440 | tf_op jit(solution)/shard_map/cond/branch_0_fun/ppermute | solution.py:193
  85.5 5.6 %collective-permute-start.1 = (bf16[1,128,512]{2,1,0:T(8,128)(2,1)S(1)}, bf16[1,128,512]{2,1,0:T(8,128)(2,1)S(1)}, u32[]{:S(2)}, u32[]{:S(2)}) collective-permute-start(bf16[1,128,512]{2,1,0:T(8,128)(2,1)S(1)} %bitcast.64), channel_id=1, source_target_pairs={{0,2},{1,5},{2,0},{3,7},{4,6},{5,1},{6,4},{7,3},{8,10},{9,13},{10,... | collective-permute-start | bytes 393224 | tf_op jit(solution)/shard_map/cond/branch_0_fun/ppermute | solution.py:193
  91.1 6.4 %collective-permute-start.5 = (bf16[1,128,512]{2,1,0:T(8,128)(2,1)S(1)}, bf16[1,128,512]{2,1,0:T(8,128)(2,1)S(1)}, u32[]{:S(2)}, u32[]{:S(2)}) collective-permute-start(bf16[1,128,512]{2,1,0:T(8,128)(2,1)S(1)} %bitcast.68), channel_id=1, source_target_pairs={{0,8},{1,5},{2,10},{3,7},{4,12},{5,1},{6,14},{7,3},{8,0},{9,13},{1... | collective-permute-start | bytes 393224 | tf_op jit(solution)/shard_map/cond/branch_0_fun/ppermute | solution.py:193
  91.2 7.5 %collective-permute-start.2 = (bf16[2,128,512]{2,1,0:T(8,128)(2,1)S(1)}, bf16[2,128,512]{2,1,0:T(8,128)(2,1)S(1)}, u32[]{:S(2)}, u32[]{:S(2)}) collective-permute-start(bf16[2,128,512]{2,1,0:T(8,128)(2,1)S(1)} %pad_maximum_fusion.2), channel_id=1, source_target_pairs={{0,4},{1,9},{2,6},{3,11},{4,0},{5,13},{6,2},{7,15},{8,12},{9,1},{1... | collective-permute-start | bytes 786440 | tf_op jit(solution)/shard_map/cond/branch_0_fun/ppermute | solution.py:193
  97.5 9.2 %collective-permute-start.6 = (bf16[2,128,512]{2,1,0:T(8,128)(2,1)S(1)}, bf16[2,128,512]{2,1,0:T(8,128)(2,1)S(1)}, u32[]{:S(2)}, u32[]{:S(2)}) collective-permute-start(bf16[2,128,512]{2,1,0:T(8,128)(2,1)S(1)} %pad_maximum_fusion.3), channel_id=1, source_target_pairs={{0,2},{1,9},{2,0},{3,11},{4,6},{5,13},{6,4},{7,15},{8,10},{9,1},{1... | collective-permute-start | bytes 786440 | tf_op jit(solution)/shard_map/cond/branch_0_fun/ppermute | solution.py:193
  98.8 9.2 %collective-permute-start.3 = (bf16[4,128,512]{2,1,0:T(8,128)(2,1)S(1)}, bf16[4,128,512]{2,1,0:T(8,128)(2,1)S(1)}, u32[]{:S(2)}, u32[]{:S(2)}) collective-permute-start(bf16[4,128,512]{2,1,0:T(8,128)(2,1)S(1)} %pad_maximum_fusion), channel_id=1, source_target_pairs={{0,8},{1,3},{2,10},{3,1},{4,12},{5,7},{6,14},{7,5},{8,0},{9,11},{1... | collective-permute-start | bytes 1572872 | tf_op jit(solution)/shard_map/cond/branch_0_fun/ppermute | solution.py:193
  106.8 9.2 %collective-permute-start.7 = (bf16[4,128,512]{2,1,0:T(8,128)(2,1)S(1)}, bf16[4,128,512]{2,1,0:T(8,128)(2,1)S(1)}, u32[]{:S(2)}, u32[]{:S(2)}) collective-permute-start(bf16[4,128,512]{2,1,0:T(8,128)(2,1)S(1)} %pad_maximum_fusion.1), channel_id=1, source_target_pairs={{0,4},{1,3},{2,6},{3,1},{4,0},{5,7},{6,2},{7,5},{8,12},{9,11},{10,... | collective-permute-start | bytes 1572872 | tf_op jit(solution)/shard_map/cond/branch_0_fun/ppermute | solution.py:193

commit v4 on v3

--- a/solution.py
+++ b/solution.py
@@ -21,33 +21,36 @@
 
 
 def opening(chunks, place, tokens, centroids, prices, kept, sent, mine, *refs):
-    parcels, (tok, cen, acc, sem) = refs[:-4], refs[-4:]
+    parcels, (tok, cen, cost, acc, sem) = refs[:-5], refs[-5:]
     rows, cols = kept.shape[0], mine.shape[1]
-    step = tok.shape[1] // chunks
-    copies = []
-    for i in range(chunks):
-        part = pl.ds(i * step, step)
-        copies.append((
-            pltpu.make_async_copy(tokens.at[:, part], tok.at[:, part], sem.at[0, i]),
-            pltpu.make_async_copy(centroids.at[:, part], cen.at[:, part], sem.at[1, i]),
-        ))
-    for pair in copies:
-        pair[0].start()
-        pair[1].start()
-    for i, pair in enumerate(copies):
-        pair[0].wait()
-        pair[1].wait()
+
+    def pieces(source, target, which):
+        step = source.shape[0] // chunks
+        return [
+            pltpu.make_async_copy(
+                source.at[pl.ds(i * step, step)], target.at[pl.ds(i * step, step)], sem.at[which, i]
+            )
+            for i in range(chunks)
+        ]
+
+    first = pieces(centroids, cen, 0)
+    second = pieces(tokens, tok, 1)
+    third = pltpu.make_async_copy(prices, cost, sem.at[2, 0])
+    for copy in first + second + [third]:
+        copy.start()
+    for copy in first:
+        copy.wait()
+    step = tok.shape[0] // chunks
+    for i, copy in enumerate(second):
+        copy.wait()
         part = slice(i * step, (i + 1) * step)
-        product = lax.dot_general(
-            tok[:, part], cen[:, part], (((1,), (1,)), ((), ())), preferred_element_type=jnp.float32
+        acc[part, :] = lax.dot_general(
+            tok[part, :], cen[...], (((1,), (1,)), ((), ())), preferred_element_type=jnp.float32
         )
-        if i:
-            acc[...] += product
-        else:
-            acc[...] = product
+    third.wait()
     for out, at in ((sent, 1), (kept, 0)):
         row = pl.multiple_of(place[at] * rows, rows)
-        out[...] = acc[pl.ds(row, rows), :] * 0.015625 - prices[...]
+        out[...] = acc[pl.ds(row, rows), :] * 0.015625 - cost[...]
     mine[...] = cen[:, pl.ds(pl.multiple_of(place[2] * cols, cols), cols)]
     for k, parcel in enumerate(parcels):
         parcel[...] = tok[:, pl.ds(pl.multiple_of(place[3 + k] * cols, cols), cols)]
@@ -104,7 +107,8 @@
 
 
 def finish(ne, rows, outer, place, info, before, prices, *refs):
-    columns, (final, holder, best, counts_out, fits, *sums) = refs[: -5 - 2], refs[-5 - 2 :]
+    columns, (final, holder, best, counts_out, fits, *sums) = refs[: -5 - 4], refs[-5 - 4 :]
+    sums, short = sums[:2], sums[2:]
     experts = before.shape[1]
     own = prices.shape[1]
     start = place[0]
@@ -125,7 +129,8 @@
         holder[...] = jnp.where(top_bid > 0, jnp.min(firsts, axis=0), -1.0).astype(jnp.int32)
     at = 3 * experts
     for c in range(ne):
-        best[c] = info[place[1] * ne + c, :, at : at + rows].astype(jnp.int32)
+        mark = info[place[1] * ne + c, :, at : at + rows]
+        best[:, c * rows : (c + 1) * rows] = mark.astype(jnp.int32)
     ids = (start + lax.broadcasted_iota(jnp.int32, (own, rows), 0)).astype(jnp.float32)
     total = jnp.zeros((own, sums[0].shape[1]), jnp.float32)
     for k, features in enumerate(columns):
@@ -136,8 +141,9 @@
                 hot, features[c * rows : (c + 1) * rows, :], preferred_element_type=jnp.float32
             )
     part = own // len(sums)
-    for i, out in enumerate(sums):
+    for i, (out, brief) in enumerate(zip(sums, short)):
         out[...] = total[i * part : (i + 1) * part]
+        brief[...] = total[i * part : (i + 1) * part].astype(brief.dtype)
     share = info.shape[0] // outer
     parts = [
         jnp.sum(info[i * share : (i + 1) * share, :, 2 * experts : at], axis=0) for i in range(outer)
@@ -162,16 +168,15 @@
 
 
 def assemble(plan, base, *refs):
-    pieces, out, sem = refs[:-2], refs[-2], refs[-1]
+    pieces, out, sem = refs[: len(plan)], refs[-2], refs[-1]
     rows, cols = pieces[0].shape[-2:]
     copies = []
     for piece, (row, slots) in zip(pieces, plan):
         for i, slot in enumerate(slots):
             col = pl.multiple_of(base[slot] * cols, cols)
-            source = piece if len(piece.shape) == 2 else piece.at[i]
             copies.append(
                 pltpu.make_async_copy(
-                    source, out.at[pl.ds(row, rows), pl.ds(col, cols)], sem.at[len(copies)]
+                    piece.at[i], out.at[pl.ds(row, rows), pl.ds(col, cols)], sem.at[len(copies)]
                 )
             )
     for copy in copies:
@@ -183,7 +188,7 @@
 TURNS = ((0, 1), (2, 1))
 
 
-def spread_out(dp, inner, wide, sums, mine, counts):
+def spread_out(dp, inner, wide, sums, short, mine, counts):
     bits = inner.bit_length() - 1
     member = lax.axis_index("dp") % inner
     core = lax.axis_index("expert")
@@ -194,9 +199,9 @@
 
     parts = len(sums)
     rows, cols = sums[0].shape
-    sent = [s if wide else s.astype(jnp.bfloat16) for s in sums]
+    sent = sums if wide else short
     other = [move(s, (inner, inner)) for s in sent] if inner < dp else None
-    held, pieces, plan, slots = [], [], [], []
+    held = []
     for p in range(parts):
         terms = [sums[p], other[p]] if other else [sums[p]]
         fresh = pl.pallas_call(
@@ -208,29 +213,46 @@
             name="blend",
         )(mine, counts, *terms)
         held.append([(fresh[None], [(0, 0)])])
+
+    def join(values):
+        return values[0] if len(values) == 1 else jnp.concatenate(values)
+
+    late = [[] for _ in range(parts)]
     for stage in range(bits):
         for p in range(parts):
-            turns = [(stage + t) % bits for t in TURNS[p]]
-            masks = [1 << t for t in turns]
-            values = [v for v, _ in held[p]]
-            where = [m for _, ms in held[p] for m in ms]
-            value = values[0] if len(values) == 1 else jnp.concatenate(values)
-            held[p].append((move(value, masks), [(a ^ masks[0], b ^ masks[1]) for a, b in where]))
-    for p in range(parts):
-        for value, where in held[p]:
-            pieces.append(value)
-            plan.append((p * rows, [len(slots) + i for i in range(len(where))]))
-            slots += where
-    base = jnp.stack([member ^ jnp.where(core == 0, a, b) for a, b in slots]).astype(jnp.int32)
-    return pl.pallas_call(
-        functools.partial(assemble, plan),
-        out_shape=jax.ShapeDtypeStruct((parts * rows, inner * cols), mine.dtype),
-        in_specs=[SMEM] + [VMEM] * len(pieces),
-        out_specs=ANY,
-        scratch_shapes=[pltpu.SemaphoreType.DMA((len(slots),))],
-        compiler_params=room(16),
-        name="assemble",
-    )(base, *pieces)
+            masks = [1 << (stage + t) % bits for t in TURNS[p]]
+
+            def onward(entries):
+                where = [m for _, ms in entries for m in ms]
+                value = move(join([v for v, _ in entries]), masks)
+                return value, [(a ^ masks[0], b ^ masks[1]) for a, b in where]
+
+            if stage < bits - 1 or stage < 2:
+                held[p].append(onward(held[p]))
+            else:
+                late[p] = [onward(held[p][:-1]), onward(held[p][-1:])]
+    def write(whole, groups):
+        pieces, plan, slots = [], [], []
+        for p, group in enumerate(groups):
+            for value, where in group:
+                pieces.append(value)
+                plan.append((p * rows, [len(slots) + i for i in range(len(where))]))
+                slots += where
+        base = jnp.stack([member ^ jnp.where(core == 0, a, b) for a, b in slots]).astype(jnp.int32)
+        before = [] if whole is None else [whole]
+        return pl.pallas_call(
+            functools.partial(assemble, plan),
+            out_shape=jax.ShapeDtypeStruct((parts * rows, inner * cols), mine.dtype),
+            in_specs=[SMEM] + [VMEM] * len(pieces) + [ANY] * len(before),
+            out_specs=ANY,
+            scratch_shapes=[pltpu.SemaphoreType.DMA((len(slots),))],
+            input_output_aliases={1 + len(pieces): 0} if before else {},
+            compiler_params=room(16),
+            name="assemble",
+        )(base, *pieces, *before)
+
+    whole = write(None, held)
+    return write(whole, late) if any(late) else whole
 
 
 def body(dp, ne, tokens, centroids, prices, epsilon):
@@ -265,15 +287,16 @@
             out_shape=[shape(rows, own)] * 2
             + [shape(own, cols, dtype=centroids.dtype)]
             + [shape(local_tokens, cols, dtype=tokens.dtype)] * half,
-            in_specs=[SMEM, ANY, ANY, VMEM],
+            in_specs=[SMEM, ANY, ANY, ANY],
             out_specs=[VMEM] * (3 + half),
             scratch_shapes=[
                 pltpu.VMEM(tokens.shape, tokens.dtype),
                 pltpu.VMEM(centroids.shape, centroids.dtype),
+                pltpu.VMEM((1, own), f32),
                 pltpu.VMEM((local_tokens, own), f32),
-                pltpu.SemaphoreType.DMA((2, chunks)),
+                pltpu.SemaphoreType.DMA((3, chunks)),
             ],
-            compiler_params=room(48),
+            compiler_params=room(52),
             name="opening",
         )(place, tokens, centroids, prices.reshape(1, own))
         received = lax.ppermute(sent, "expert", swap)
@@ -291,7 +314,6 @@
                 (i * 2 + c, (i ^ (2 * k + c)) * 2 + c) for i in range(dp) for c in range(2)
             ]
             columns.append(lax.ppermute(parcel, everywhere, pairs))
-        columns += [lax.ppermute(c, "expert", swap) for c in columns]
         sources = theirs + [dp_at ^ (2 * k + 1 - expert_at) for k in range(half)]
     else:
         parcels = tokens.reshape(local_tokens, dp, cols).transpose(1, 0, 2)
@@ -323,7 +345,11 @@
             compiler_params=room(4),
             name="next_round",
         )(values, total, epsilon, bids)
+    if paired:
+        total, columns = lax.optimization_barrier((total, columns))
+        columns += [lax.ppermute(c, "expert", swap) for c in columns]
     bids = lax.all_to_all(bids, everywhere, 0, 0, tiled=True)
+    bids, columns = lax.optimization_barrier((bids, columns))
     wide = (rows // 128 + 1) * 128
     largest = jnp.max(jnp.abs(tokens)).astype(f32).reshape(1)
     base = (dp_at * local_tokens + expert_at * rows).astype(jnp.int32).reshape(1)
@@ -345,21 +371,22 @@
         out_shape=(
             shape(1, listed),
             shape(1, listed, dtype=jnp.int32),
-            shape(ne, 1, rows, dtype=jnp.int32),
+            shape(1, local_tokens, dtype=jnp.int32),
             shape(own, 128),
             shape(1, dtype=jnp.int32),
         )
-        + (shape(own // 2, cols),) * 2,
+        + (shape(own // 2, cols),) * 2
+        + (shape(own // 2, cols, dtype=jnp.bfloat16),) * 2,
         in_specs=[SMEM] + [VMEM] * (3 + len(columns)),
-        out_specs=(VMEM, VMEM, VMEM, VMEM, SMEM, VMEM, VMEM),
+        out_specs=(VMEM, VMEM, VMEM, VMEM, SMEM) + (VMEM,) * 4,
         compiler_params=room(16),
         name="finish",
     )(place, info, total, prices.reshape(1, own), *columns)
     if paired:
         spread_as = [functools.partial(spread_out, dp, inner, wide) for wide in (True, False)]
-        refreshed = lax.cond(fits[0] > 0, spread_as[1], spread_as[0], sums, mine, counts)
+        refreshed = lax.cond(fits[0] > 0, spread_as[1], spread_as[0], sums[:2], sums[2:], mine, counts)
     else:
-        sums = jnp.concatenate(sums)
+        sums = jnp.concatenate(sums[:2])
         fresh = 0.5 * mine.astype(f32) + 0.5 * sums / counts[:, :1]
         refreshed = lax.all_gather(fresh.astype(centroids.dtype), "dp", axis=1, tiled=True)
     if direct:
@@ -367,7 +394,7 @@
     else:
         final = prices + lax.dynamic_slice_in_dim(final[0], expert_at * own, own, 0)
         holder = lax.dynamic_slice_in_dim(holder[0], expert_at * own, own, 0)
-    return final, best.reshape(local_tokens), holder, refreshed
+    return final, best[0], holder, refreshed
 
 
 def solution(mesh):

time: 119 us -> 117 us (0.983)
  blocking collectives: 0 us -> 18.7 us
  waiting for transfers between devices: 64.3 us -> 46.7 us
  starting transfers between devices: 30.1 us -> 23.7 us
  Pallas kernels: 14.5 us -> 18.2 us
    all_to_all x0 -> x1, blocking collectives: none -> 18.7 us  [body(): bids = lax.all_to_all(bids, everywhere, 0, 0, tiled=True)]
    all_to_all x2 -> x1, waiting for transfers between devices: 13.1 us -> 3.69 us  [body(): bids = lax.all_to_all(bids, everywhere, 0, 0, tiled=True)]
    ppermute x8 -> x10, waiting for transfers between devices: 42.2 us -> 32.9 us  [move(): return lax.ppermute(value, ('dp', 'expert'), pairs)]
    all_to_all x2 -> x1, starting transfers between devices: 12 us -> 4.02 us  [body(): bids = lax.all_to_all(bids, everywhere, 0, 0, tiled=True)]
    pallas_call x1, Pallas kernels: 4.74 us -> 8.3 us  [body(): pl.pallas_call(functools.partial(opening, chunks), out_shape=[shape(rows,...]
    all_to_all x1, waiting for transfers between devices: 6.33 us -> 9.72 us  [body(): info = lax.all_to_all(info, everywhere, 0, 0, tiled=True)]
    ppermute x4, waiting for transfers between devices: 2.29 us -> 0.01 us  [body(): columns += [lax.ppermute(c, 'expert', swap) for c in columns]]
    ppermute x1, starting transfers between devices: 0.51 us -> 2.61 us  [body(): received = lax.ppermute(sent, 'expert', swap)]
  transfers between devices with their start and end apart: 20 -> 21, of which waited for: 14 -> 11; matrix products, arithmetic and copies ran while one was open for 3% -> 3% of each run, Pallas kernels for 4% -> 4%
where the time goes in v4:
time: 117 us; the launch traced here: 116 us
  waiting for transfers between devices  46.7 us (40%)
  starting transfers between devices  23.7 us (20%)
  blocking collectives  18.7 us (16%)
  Pallas kernels  18.2 us (16%)
  other arithmetic  3.64 us (3%)
  between operations  2.83 us (2%)
  local copies, waits for them, and re-layouts  2.33 us (2%)
    ppermute x10, waiting for transfers between devices, move(): return lax.ppermute(value, ('dp', 'expert'), pairs)  32.9 us
    all_to_all x1, blocking collectives, body(): bids = lax.all_to_all(bids, everywhere, 0, 0, tiled=True)  18.7 us
    all_to_all x1, waiting for transfers between devices, body(): info = lax.all_to_all(info, everywhere, 0, 0, tiled=True)  9.72 us
    pallas_call x1, Pallas kernels, body(): pl.pallas_call(functools.partial(opening, chunks), out_shape=[shape(rows,...  8.3 us
    ppermute x10, starting transfers between devices, move(): return lax.ppermute(value, ('dp', 'expert'), pairs)  8.07 us
    ppermute x4, starting transfers between devices, body(): columns.append(lax.ppermute(parcel, everywhere, pairs))  5.3 us
    all_to_all x1, starting transfers between devices, body(): bids = lax.all_to_all(bids, everywhere, 0, 0, tiled=True)  4.02 us
    all_to_all x1, waiting for transfers between devices, body(): bids = lax.all_to_all(bids, everywhere, 0, 0, tiled=True)  3.69 us
  transfers between devices with their start and end apart: 21, of which 11 were waited for; matrix products, arithmetic and copies ran while one was open for 3% of the time, Pallas kernels for 4%

profile of v4, /device:TPU:0, one launch (start us, length us, event | category | flops | bytes accessed | tf_op | source)
XLA Modules:
  0.0 116.2 jit_solution(2440017466023494126)
XLA Ops:
  0.7 0.1 stack.176.place
  0.8 0.7 copy-done.2
  1.5 8.3 %opening.1 = (f32[192,256]{1,0:T(8,128)S(1)}, f32[192,256]{1,0:T(8,128)S(1)}, bf16[256,512]{1,0:T(8,128)(2,1)}, bf16[384,512]{1,0:T(8,128)(2,1)S(1)}, bf16[384,5...) custom-call(s32[7]{0:T(128)S(1)} %stack.176.place, bf16[384,4096]{1,0:T(8,128)(2,1)} %tokens.1, ...), custom_call_target="tpu_custom_call" | custom-call | tf_op jit(solution)/shard_map/opening/pallas_call | solution.py:285
  9.8 0.7 collective-permute-start.21
  10.5 3.0 %collective-permute-start.22 = (bf16[384,512]{1,0:T(8,128)(2,1)S(1)}, bf16[384,512]{1,0:T(8,128)(2,1)S(1)}, u32[]{:S(2)}, u32[]{:S(2)}) collective-permute-start(bf16[384,512]{1,0:T(8,128)(2,1)S(1)} %get-tuple-element.79), channel_id=1, source_target_pairs={{0,4},{1,7},{2,6},{3,5},{4,0},{5,3},{6,2},{7,1},{8,12},{9,15},{10,... | collective-permute-start | bytes 1179656 | tf_op jit(solution)/shard_map/ppermute | solution.py:316
  13.5 1.6 %collective-permute-start.23 = (bf16[384,512]{1,0:T(8,128)(2,1)S(1)}, bf16[384,512]{1,0:T(8,128)(2,1)S(1)}, u32[]{:S(2)}, u32[]{:S(2)}) collective-permute-start(bf16[384,512]{1,0:T(8,128)(2,1)S(1)} %get-tuple-element.80), channel_id=1, source_target_pairs={{0,8},{1,11},{2,10},{3,9},{4,12},{5,15},{6,14},{7,13},{8,0},{9,3},... | collective-permute-start | bytes 1179656 | tf_op jit(solution)/shard_map/ppermute | solution.py:316
  15.1 2.6 %collective-permute-start.20 = (f32[192,256]{1,0:T(8,128)S(1)}, f32[192,256]{1,0:T(8,128)S(1)}, u32[]{:S(2)}, u32[]{:S(2)}) collective-permute-start(f32[192,256]{1,0:T(8,128)S(1)} %get-tuple-element.74), channel_id=1, source_target_pairs={{0,1},{1,0},{2,3},{3,2},{4,5},{5,4},{6,7},{7,6},{8,9},{9,8},{10,11... | collective-permute-start | bytes 589832 | tf_op jit(solution)/shard_map/ppermute | solution.py:302
  18.4 0.4 collective-permute-done.20.theirs
  18.8 0.3 first_round.1
  19.1 18.7 %all_to_all.15.bids = f32[32,1,512]{2,1,0:T(1,128)S(1)} all-to-all(f32[32,1,512]{2,1,0:T(1,128)S(1)} %get-tuple-element.76), channel_id=1, replica_groups=mesh['dp'=16,'expert'=2] {'dp','expert'}, dimensions={0} | all-to-all | bytes 131072 | tf_op jit(solution)/shard_map/all_to_all | solution.py:339
  37.8 0.3 next_round.1
  38.1 0.6 copy-done.1
  38.8 0.1 collective-permute-start.25
  38.9 0.5 collective-permute-start.26
  39.4 0.1 collective-permute-start.27
  39.4 0.4 collective-permute-start.28
  39.9 4.0 %all-to-all-start.1 = ((f32[32,1,512]{2,1,0:T(1,128)}), f32[32,1,512]{2,1,0:T(1,128)}, u32[]{:S(2)}, u32[]{:S(2)}) async-start(f32[32,1,512]{2,1,0:T(1,128)} %copy-done.1), calls=%async_computation.1 | async-start | bytes 131072 | tf_op jit(solution)/shard_map/all_to_all | solution.py:351
  43.9 3.0 %abs_reduce_fusion = bf16[]{:T(256)} fusion(bf16[384,4096]{1,0:T(8,128)(2,1)} %tokens.1), kind=kLoop, calls=%fused_computation.4 | loop fusion | flops 3145727 | bytes 3145730 | tf_op jit(solution)/shard_map/reduce_max | solution.py:354
  47.6 3.7 %all-to-all-done.1.bids = f32[32,1,512]{2,1,0:T(1,128)} async-done(((f32[32,1,512]{2,1,0:T(1,128)}), f32[32,1,512]{2,1,0:T(1,128)}, u32[]{:S(2)}, u32[]{:S(2)}) %all-to-all-start.1) | async-done | bytes 65568 | tf_op jit(solution)/shard_map/all_to_all | solution.py:351
  51.3 1.3 %last_round.1 = (f32[32,1,1792]{2,1,0:T(1,128)S(1)}, f32[1,512]{1,0:T(1,128)S(1)}) custom-call(f32[192,512]{1,0:T(8,128)S(1)} %get-tuple-element.75.values, f32[1,512]{1,0:T(1,128)S(1)} %get-tuple-element.82.before, f32[1]{0:T(128)S(6)} %copy.14.epsilon, f32[32,1,512]{2,1,0:T(1,128)} %all-to-all-done.1.bids, s32[1]{0:T(128)} %bitcast.50.base, ...), custom_call_target="tpu_custom_call" | custom-call | tf_op jit(solution)/shard_map/last_round/pallas_call | solution.py:356
  52.6 0.7 copy-done
  53.3 2.6 %all-to-all-start.2 = ((f32[32,1,1792]{2,1,0:T(1,128)}), f32[32,1,1792]{2,1,0:T(1,128)S(1)}, u32[]{:S(2)}, u32[]{:S(2)}) async-start(f32[32,1,1792]{2,1,0:T(1,128)} %copy-done), calls=%async_computation.2 | async-start | bytes 458752 | tf_op jit(solution)/shard_map/all_to_all | solution.py:364
  55.9 0.1 stack.168.place
  56.0 9.7 %all-to-all-done.2.info = f32[32,1,1792]{2,1,0:T(1,128)S(1)} async-done(((f32[32,1,1792]{2,1,0:T(1,128)}), f32[32,1,1792]{2,1,0:T(1,128)S(1)}, u32[]{:S(2)}, u32[]{:S(2)}) %all-to-all-start.2) | async-done | bytes 229408 | tf_op jit(solution)/shard_map/all_to_all | solution.py:364
  65.7 2.6 %finish.1 = (f32[1,256]{1,0:T(1,128)}, s32[1,256]{1,0:T(1,128)}, s32[1,384]{1,0:T(1,128)S(1)}, f32[256,128]{1,0:T(8,128)S(1)}, s32[1]{0:T(128)}, /*index=5*/f32[...) custom-call(s32[10]{0:T(128)S(1)} %stack.168.place, ...), custom_call_target="tpu_custom_call" | custom-call | tf_op jit(solution)/shard_map/finish/pallas_call | solution.py:369
  69.0 0.6 reduce
  69.6 46.6 %conditional.1 = (bf16[256,4096]{1,0:T(8,128)(2,1)}) conditional(s32[]{:T(128)} %bitcast.54, (f32[128,512]{1,0:T(8,128)}, bf16[256,512]{1,0:T(8,128)(2,1)}, f32[256,128]{1,0:T(8,128)S(1)}, f32[128,512]{1,0:T(8,128)}) %tuple.18, (bf16[128,512]{1,0:T(8,128)(2,1)}, bf16[256,512]{1,0:T(8,128)(2,1)}, f32[256,128]{1,0:T(8,128)S(1)}, f32[128,512]{1,0:T(8,128)}, ...), branch_computations={%region_1.2_spmd, %region_2.3_spmd} | conditional | flops 262186 | bytes 10486778 | solution.py:387
  69.6 0.6 collective-permute-start.5
  70.2 2.3 %collective-permute-start = (f32[128,512]{1,0:T(8,128)}, f32[128,512]{1,0:T(8,128)S(1)}, u32[]{:S(2)}, u32[]{:S(2)}) collective-permute-start(f32[128,512]{1,0:T(8,128)} %get-tuple-element.25.refs_0_), channel_id=1, source_target_pairs={{0,16},{1,17},{2,18},{3,19},{4,20},{5,21},{6,22},{7,23},{8,24},{9,... | collective-permute-start | bytes 786440 | tf_op jit(solution)/shard_map/cond/branch_0_fun/ppermute | solution.py:198
  72.5 17.5 %collective-permute-done.5.refs_1_ = f32[128,512]{1,0:T(8,128)S(1)} collective-permute-done((f32[128,512]{1,0:T(8,128)}, f32[128,512]{1,0:T(8,128)S(1)}, u32[]{:S(2)}, u32[]{:S(2)}) %collective-permute-start.5) | collective-permute-done | bytes 262176 | tf_op jit(solution)/shard_map/cond/branch_0_fun/ppermute | solution.py:198
  90.0 1.1 blend.5
  91.2 4.4 %collective-permute-done.refs_1_ = f32[128,512]{1,0:T(8,128)S(1)} collective-permute-done((f32[128,512]{1,0:T(8,128)}, f32[128,512]{1,0:T(8,128)S(1)}, u32[]{:S(2)}, u32[]{:S(2)}) %collective-permute-start) | collective-permute-done | bytes 262176 | tf_op jit(solution)/shard_map/cond/branch_0_fun/ppermute | solution.py:198
  95.6 1.1 blend.4
  96.8 1.2 %collective-permute-start.1 = (bf16[1,128,512]{2,1,0:T(8,128)(2,1)S(1)}, bf16[1,128,512]{2,1,0:T(8,128)(2,1)S(1)}, u32[]{:S(2)}, u32[]{:S(2)}) collective-permute-start(bf16[1,128,512]{2,1,0:T(8,128)(2,1)S(1)} %bitcast.65), channel_id=1, source_target_pairs={{0,2},{1,5},{2,0},{3,7},{4,6},{5,1},{6,4},{7,3},{8,10},{9,13},{10,... | collective-permute-start | bytes 393224 | tf_op jit(solution)/shard_map/cond/branch_0_fun/ppermute | solution.py:198
  98.0 1.0 collective-permute-start.8
  98.9 2.8 %collective-permute-done.1.refs_1_ = bf16[1,128,512]{2,1,0:T(8,128)(2,1)S(1)} collective-permute-done((bf16[1,128,512]{2,1,0:T(8,128)(2,1)S(1)}, bf16[1,128,512]{2,1,0:T(8,128)(2,1)S(1)}, u32[]{:S(2)}, u32[]{:S(2)}) %collective-permute-start.1) | collective-permute-done | bytes 131104 | tf_op jit(solution)/shard_map/cond/branch_0_fun/ppermute | solution.py:198
  101.8 0.6 collective-permute-start.3
  102.4 1.5 %collective-permute-start.7 = (bf16[2,128,512]{2,1,0:T(8,128)(2,1)S(1)}, bf16[2,128,512]{2,1,0:T(8,128)(2,1)S(1)}, u32[]{:S(2)}, u32[]{:S(2)}) collective-permute-start(bf16[2,128,512]{2,1,0:T(8,128)(2,1)S(1)} %pad_maximum_fusion.1), channel_id=1, source_target_pairs={{0,4},{1,3},{2,6},{3,1},{4,0},{5,7},{6,2},{7,5},{8,12},{9,11},{10,... | collective-permute-start | bytes 786440 | tf_op jit(solution)/shard_map/cond/branch_0_fun/ppermute | solution.py:198
  103.9 1.6 %collective-permute-done.8.refs_5_ = bf16[2,128,512]{2,1,0:T(8,128)(2,1)S(1)} collective-permute-done((bf16[2,128,512]{2,1,0:T(8,128)(2,1)S(1)}, bf16[2,128,512]{2,1,0:T(8,128)(2,1)S(1)}, u32[]{:S(2)}, u32[]{:S(2)}) %collective-permute-start.8) | collective-permute-done | bytes 262176 | tf_op jit(solution)/shard_map/cond/branch_0_fun/ppermute | solution.py:198
  105.5 0.8 collective-permute-start.9
  106.3 2.0 %collective-permute-done.3.refs_2_ = bf16[2,128,512]{2,1,0:T(8,128)(2,1)S(1)} collective-permute-done((bf16[2,128,512]{2,1,0:T(8,128)(2,1)S(1)}, bf16[2,128,512]{2,1,0:T(8,128)(2,1)S(1)}, u32[]{:S(2)}, u32[]{:S(2)}) %collective-permute-start.3) | collective-permute-done | bytes 262176 | tf_op jit(solution)/shard_map/cond/branch_0_fun/ppermute | solution.py:198
  108.3 0.1 stack.122.base
  108.3 0.1 stack.114.base
  108.4 1.6 %assemble.4.refs_4_ = bf16[256,4096]{1,0:T(8,128)(2,1)} custom-call(s32[8]{0:T(128)S(1)} %stack.122.base, bf16[1,128,512]{2,1,0:T(8,128)(2,1)S(1)} %bitcast.67, bf16[1,128,512]{2,1,0:T(8,128)(2,1)S(1)} %collective-permute-done.1.refs_1_, bf16[2,128,512]{2,1,0:T(8,128)(2,1)S(1)} %collective-permute-done.3.refs_2_, bf16[1,128,512]{2,1,0:T(8,128)(2,1)S(1)} %bitcast.64, ...), custom_call_target="tpu_custom_call" | custom-call | tf_op jit(solution)/shard_map/cond/branch_0_fun/assemble/pallas_call | solution.py:243
  110.0 1.1 collective-permute-done.7.refs_2_
  111.1 2.8 %collective-permute-done.9.refs_3_ = bf16[2,128,512]{2,1,0:T(8,128)(2,1)S(1)} collective-permute-done((bf16[2,128,512]{2,1,0:T(8,128)(2,1)S(1)}, bf16[2,128,512]{2,1,0:T(8,128)(2,1)S(1)}, u32[]{:S(2)}, u32[]{:S(2)}) %collective-permute-start.9) | collective-permute-done | bytes 262176 | tf_op jit(solution)/shard_map/cond/branch_0_fun/ppermute | solution.py:198
  113.9 0.8 collective-permute-done.4.refs_1_
  114.6 1.6 %assemble.5 = bf16[256,4096]{1,0:T(8,128)(2,1)} custom-call(s32[8]{0:T(128)S(1)} %stack.114.base, bf16[2,128,512]{2,1,0:T(8,128)(2,1)S(1)} %collective-permute-done.2.refs_0_, bf16[2,128,512]{2,1,0:T(8,128)(2,1)S(1)} %collective-permute-done.4.refs_1_, bf16[2,128,512]{2,1,0:T(8,128)(2,1)S(1)} %collective-permute-done.7.refs_2_, ...), custom_call_target="tpu_custom_call", output_to_operand_aliasing={{}: (5, {})} | custom-call | tf_op jit(solution)/shard_map/cond/branch_0_fun/assemble/pallas_call | solution.py:243
  (22 shorter events, 0.2 us)
Async XLA Ops:
  0.8 0.7 copy-start.2
  9.8 29.0 %collective-permute-start.21 = (bf16[384,512]{1,0:T(8,128)(2,1)S(1)}, bf16[384,512]{1,0:T(8,128)(2,1)S(1)}, u32[]{:S(2)}, u32[]{:S(2)}) collective-permute-start(bf16[384,512]{1,0:T(8,128)(2,1)S(1)} %get-tuple-element.78), channel_id=1, source_target_pairs={{0,0},{1,3},{2,2},{3,1},{4,4},{5,7},{6,6},{7,5},{8,8},{9,11},{10,1... | collective-permute-start | bytes 1179656 | tf_op jit(solution)/shard_map/ppermute | solution.py:316
  10.5 28.3 %collective-permute-start.22 = (bf16[384,512]{1,0:T(8,128)(2,1)S(1)}, bf16[384,512]{1,0:T(8,128)(2,1)S(1)}, u32[]{:S(2)}, u32[]{:S(2)}) collective-permute-start(bf16[384,512]{1,0:T(8,128)(2,1)S(1)} %get-tuple-element.79), channel_id=1, source_target_pairs={{0,4},{1,7},{2,6},{3,5},{4,0},{5,3},{6,2},{7,1},{8,12},{9,15},{10,... | collective-permute-start | bytes 1179656 | tf_op jit(solution)/shard_map/ppermute | solution.py:316
  13.5 25.3 %collective-permute-start.23 = (bf16[384,512]{1,0:T(8,128)(2,1)S(1)}, bf16[384,512]{1,0:T(8,128)(2,1)S(1)}, u32[]{:S(2)}, u32[]{:S(2)}) collective-permute-start(bf16[384,512]{1,0:T(8,128)(2,1)S(1)} %get-tuple-element.80), channel_id=1, source_target_pairs={{0,8},{1,11},{2,10},{3,9},{4,12},{5,15},{6,14},{7,13},{8,0},{9,3},... | collective-permute-start | bytes 1179656 | tf_op jit(solution)/shard_map/ppermute | solution.py:316
  15.1 23.7 %collective-permute-start.24 = (bf16[384,512]{1,0:T(8,128)(2,1)S(1)}, bf16[384,512]{1,0:T(8,128)(2,1)S(1)}, u32[]{:S(2)}, u32[]{:S(2)}) collective-permute-start(bf16[384,512]{1,0:T(8,128)(2,1)S(1)} %get-tuple-element.81), channel_id=1, source_target_pairs={{0,12},{1,15},{2,14},{3,13},{4,8},{5,11},{6,10},{7,9},{8,4},{9,7},... | collective-permute-start | bytes 1179656 | tf_op jit(solution)/shard_map/ppermute | solution.py:316
  15.1 3.7 %collective-permute-start.20 = (f32[192,256]{1,0:T(8,128)S(1)}, f32[192,256]{1,0:T(8,128)S(1)}, u32[]{:S(2)}, u32[]{:S(2)}) collective-permute-start(f32[192,256]{1,0:T(8,128)S(1)} %get-tuple-element.74), channel_id=1, source_target_pairs={{0,1},{1,0},{2,3},{3,2},{4,5},{5,4},{6,7},{7,6},{8,9},{9,8},{10,11... | collective-permute-start | bytes 589832 | tf_op jit(solution)/shard_map/ppermute | solution.py:302
  38.1 0.6 copy-start.1
  38.8 12.5 %collective-permute-start.25 = (bf16[384,512]{1,0:T(8,128)(2,1)S(1)}, bf16[384,512]{1,0:T(8,128)(2,1)S(1)}, u32[]{:S(2)}, u32[]{:S(2)}) collective-permute-start(bf16[384,512]{1,0:T(8,128)(2,1)S(1)} %collective-permute-done.21.refs_0_), channel_id=1, source_target_pairs={{0,1},{1,0},{2,3},{3,2},{4,5},{5,4},{6,7},{7,6},{8,9},{9,8},{10,11... | collective-permute-start | bytes 1179656 | tf_op jit(solution)/shard_map/ppermute | solution.py:350
  38.9 12.4 %collective-permute-start.26 = (bf16[384,512]{1,0:T(8,128)(2,1)S(1)}, bf16[384,512]{1,0:T(8,128)(2,1)S(1)}, u32[]{:S(2)}, u32[]{:S(2)}) collective-permute-start(bf16[384,512]{1,0:T(8,128)(2,1)S(1)} %collective-permute-done.22.refs_1_), channel_id=1, source_target_pairs={{0,1},{1,0},{2,3},{3,2},{4,5},{5,4},{6,7},{7,6},{8,9},{9,8},{10,11... | collective-permute-start | bytes 1179656 | tf_op jit(solution)/shard_map/ppermute | solution.py:350
  39.4 11.9 %collective-permute-start.27 = (bf16[384,512]{1,0:T(8,128)(2,1)S(1)}, bf16[384,512]{1,0:T(8,128)(2,1)S(1)}, u32[]{:S(2)}, u32[]{:S(2)}) collective-permute-start(bf16[384,512]{1,0:T(8,128)(2,1)S(1)} %collective-permute-done.23.refs_2_), channel_id=1, source_target_pairs={{0,1},{1,0},{2,3},{3,2},{4,5},{5,4},{6,7},{7,6},{8,9},{9,8},{10,11... | collective-permute-start | bytes 1179656 | tf_op jit(solution)/shard_map/ppermute | solution.py:350
  39.4 11.9 %collective-permute-start.28 = (bf16[384,512]{1,0:T(8,128)(2,1)S(1)}, bf16[384,512]{1,0:T(8,128)(2,1)S(1)}, u32[]{:S(2)}, u32[]{:S(2)}) collective-permute-start(bf16[384,512]{1,0:T(8,128)(2,1)S(1)} %collective-permute-done.24.refs_3_), channel_id=1, source_target_pairs={{0,1},{1,0},{2,3},{3,2},{4,5},{5,4},{6,7},{7,6},{8,9},{9,8},{10,11... | collective-permute-start | bytes 1179656 | tf_op jit(solution)/shard_map/ppermute | solution.py:350
  39.9 25.8 %copy-start.3 = (f32[256]{0:T(256)S(1)}, f32[256]{0:T(256)}, u32[]{:S(2)}) copy-start(f32[256]{0:T(256)} %param.8) | copy-start | bytes 3076
  39.9 11.4 %all-to-all-start.1 = ((f32[32,1,512]{2,1,0:T(1,128)}), f32[32,1,512]{2,1,0:T(1,128)}, u32[]{:S(2)}, u32[]{:S(2)}) async-start(f32[32,1,512]{2,1,0:T(1,128)} %copy-done.1), calls=%async_computation.1 | async-start | bytes 131072 | tf_op jit(solution)/shard_map/all_to_all | solution.py:351
  52.6 0.7 copy-start
  53.3 12.4 %all-to-all-start.2 = ((f32[32,1,1792]{2,1,0:T(1,128)}), f32[32,1,1792]{2,1,0:T(1,128)S(1)}, u32[]{:S(2)}, u32[]{:S(2)}) async-start(f32[32,1,1792]{2,1,0:T(1,128)} %copy-done), calls=%async_computation.2 | async-start | bytes 458752 | tf_op jit(solution)/shard_map/all_to_all | solution.py:364
  69.6 20.4 %collective-permute-start.5 = (f32[128,512]{1,0:T(8,128)}, f32[128,512]{1,0:T(8,128)S(1)}, u32[]{:S(2)}, u32[]{:S(2)}) collective-permute-start(f32[128,512]{1,0:T(8,128)} %get-tuple-element.26.refs_0_), channel_id=1, source_target_pairs={{0,16},{1,17},{2,18},{3,19},{4,20},{5,21},{6,22},{7,23},{8,24},{9,... | collective-permute-start | bytes 786440 | tf_op jit(solution)/shard_map/cond/branch_0_fun/ppermute | solution.py:198
  70.2 25.4 %collective-permute-start = (f32[128,512]{1,0:T(8,128)}, f32[128,512]{1,0:T(8,128)S(1)}, u32[]{:S(2)}, u32[]{:S(2)}) collective-permute-start(f32[128,512]{1,0:T(8,128)} %get-tuple-element.25.refs_0_), channel_id=1, source_target_pairs={{0,16},{1,17},{2,18},{3,19},{4,20},{5,21},{6,22},{7,23},{8,24},{9,... | collective-permute-start | bytes 786440 | tf_op jit(solution)/shard_map/cond/branch_0_fun/ppermute | solution.py:198
  91.1 6.8 %collective-permute-start.6 = (bf16[1,128,512]{2,1,0:T(8,128)(2,1)S(1)}, bf16[1,128,512]{2,1,0:T(8,128)(2,1)S(1)}, u32[]{:S(2)}, u32[]{:S(2)}) collective-permute-start(bf16[1,128,512]{2,1,0:T(8,128)(2,1)S(1)} %bitcast.62), channel_id=1, source_target_pairs={{0,8},{1,5},{2,10},{3,7},{4,12},{5,1},{6,14},{7,3},{8,0},{9,13},{1... | collective-permute-start | bytes 393224 | tf_op jit(solution)/shard_map/cond/branch_0_fun/ppermute | solution.py:198
  96.8 5.0 %collective-permute-start.1 = (bf16[1,128,512]{2,1,0:T(8,128)(2,1)S(1)}, bf16[1,128,512]{2,1,0:T(8,128)(2,1)S(1)}, u32[]{:S(2)}, u32[]{:S(2)}) collective-permute-start(bf16[1,128,512]{2,1,0:T(8,128)(2,1)S(1)} %bitcast.65), channel_id=1, source_target_pairs={{0,2},{1,5},{2,0},{3,7},{4,6},{5,1},{6,4},{7,3},{8,10},{9,13},{10,... | collective-permute-start | bytes 393224 | tf_op jit(solution)/shard_map/cond/branch_0_fun/ppermute | solution.py:198
  98.0 7.5 %collective-permute-start.8 = (bf16[2,128,512]{2,1,0:T(8,128)(2,1)S(1)}, bf16[2,128,512]{2,1,0:T(8,128)(2,1)S(1)}, u32[]{:S(2)}, u32[]{:S(2)}) collective-permute-start(bf16[2,128,512]{2,1,0:T(8,128)(2,1)S(1)} %pad_maximum_fusion.1), channel_id=1, source_target_pairs={{0,2},{1,9},{2,0},{3,11},{4,6},{5,13},{6,4},{7,15},{8,10},{9,1},{1... | collective-permute-start | bytes 786440 | tf_op jit(solution)/shard_map/cond/branch_0_fun/ppermute | solution.py:198
  101.8 6.4 %collective-permute-start.3 = (bf16[2,128,512]{2,1,0:T(8,128)(2,1)S(1)}, bf16[2,128,512]{2,1,0:T(8,128)(2,1)S(1)}, u32[]{:S(2)}, u32[]{:S(2)}) collective-permute-start(bf16[2,128,512]{2,1,0:T(8,128)(2,1)S(1)} %pad_maximum_fusion), channel_id=1, source_target_pairs={{0,4},{1,9},{2,6},{3,11},{4,0},{5,13},{6,2},{7,15},{8,12},{9,1},{1... | collective-permute-start | bytes 786440 | tf_op jit(solution)/shard_map/cond/branch_0_fun/ppermute | solution.py:198
  102.4 8.6 %collective-permute-start.7 = (bf16[2,128,512]{2,1,0:T(8,128)(2,1)S(1)}, bf16[2,128,512]{2,1,0:T(8,128)(2,1)S(1)}, u32[]{:S(2)}, u32[]{:S(2)}) collective-permute-start(bf16[2,128,512]{2,1,0:T(8,128)(2,1)S(1)} %pad_maximum_fusion.1), channel_id=1, source_target_pairs={{0,4},{1,3},{2,6},{3,1},{4,0},{5,7},{6,2},{7,5},{8,12},{9,11},{10,... | collective-permute-start | bytes 786440 | tf_op jit(solution)/shard_map/cond/branch_0_fun/ppermute | solution.py:198
  103.9 7.2 %collective-permute-start.2 = (bf16[2,128,512]{2,1,0:T(8,128)(2,1)S(1)}, bf16[2,128,512]{2,1,0:T(8,128)(2,1)S(1)}, u32[]{:S(2)}, u32[]{:S(2)}) collective-permute-start(bf16[2,128,512]{2,1,0:T(8,128)(2,1)S(1)} %pad_maximum_fusion), channel_id=1, source_target_pairs={{0,8},{1,3},{2,10},{3,1},{4,12},{5,7},{6,14},{7,5},{8,0},{9,11},{1... | collective-permute-start | bytes 786440 | tf_op jit(solution)/shard_map/cond/branch_0_fun/ppermute | solution.py:198
  105.5 8.4 %collective-permute-start.9 = (bf16[2,128,512]{2,1,0:T(8,128)(2,1)S(1)}, bf16[2,128,512]{2,1,0:T(8,128)(2,1)S(1)}, u32[]{:S(2)}, u32[]{:S(2)}) collective-permute-start(bf16[2,128,512]{2,1,0:T(8,128)(2,1)S(1)} %collective-permute-done.8.refs_5_), channel_id=1, source_target_pairs={{0,4},{1,3},{2,6},{3,1},{4,0},{5,7},{6,2},{7,5},{8,12},{9,11},{10,... | collective-permute-start | bytes 786440 | tf_op jit(solution)/shard_map/cond/branch_0_fun/ppermute | solution.py:198
  108.3 6.4 %collective-permute-start.4 = (bf16[2,128,512]{2,1,0:T(8,128)(2,1)S(1)}, bf16[2,128,512]{2,1,0:T(8,128)(2,1)S(1)}, u32[]{:S(2)}, u32[]{:S(2)}) collective-permute-start(bf16[2,128,512]{2,1,0:T(8,128)(2,1)S(1)} %collective-permute-done.3.refs_2_), channel_id=1, source_target_pairs={{0,8},{1,3},{2,10},{3,1},{4,12},{5,7},{6,14},{7,5},{8,0},{9,11},{1... | collective-permute-start | bytes 786440 | tf_op jit(solution)/shard_map/cond/branch_0_fun/ppermute | solution.py:198
